TPU v7x, 32 devices: a whole 2x2x4 slice. The times are simulated.
32 devices in a mesh: dp: 4 (over y, x), zero: 8 (over z, core).
Axes of the slice: x: 2, y: 2, z: 4, core: 2. Of those that a mesh axis runs over, the one named last changes fastest.
Arguments:
- feats: bfloat16 [4096, 6144], P(('dp', 'zero')), may hold values from -6 to 6
- short_filter: bfloat16 [7, 6144], P(None, 'zero'), may hold values from -2 to 2
- medium_filter: float32 [128, 128], replicated, may hold values from -0.5 to 0.5
- doc_ids: int32 [32, 128], P(('dp', 'zero')), may hold values from 0 to 2, never falling along the last dimension, each value on 1 to 112 neighbouring positions
- counts: int32 [32], P(('dp', 'zero')), may hold values from 64 to 128
- plan: int32 [32], P(('dp', 'zero')), may hold values from 0 to 3, as said below
- cotangent: bfloat16 [4096, 2048], P(('dp', 'zero')), may hold values from -6 to 6
Outputs:
- mixed: bfloat16 [4096, 2048], P(('dp', 'zero'))
- feats_grad: bfloat16 [4096, 6144], P(('dp', 'zero'))
- short_grad: float32 [7, 6144], P(None, 'zero')
- medium_grad: float32 [128, 128], replicated
Inputs may be any that keep to these rules, and one draw needn't show every extreme that they name: `plan`: every data rank is named by some tile.
All inputs are finite; a program needn't handle non-finite values.
Results may differ from a plain program's by a relative error of at most 0.0058.
Values may be sent and summed in bfloat16 or wider, within the bound.
A program may use at most 64 MiB of HBM per device.

v0:
```python
import jax
import jax.numpy as jnp
from jax import lax
from jax.sharding import PartitionSpec as P

SHORT = 7


def shift_down(values, offset):
    return jnp.concatenate(
        [jnp.zeros((offset, values.shape[1]), values.dtype), values[: values.shape[0] - offset]], 0
    )


def shift_up(values, offset):
    return jnp.concatenate([values[offset:], jnp.zeros((offset, values.shape[1]), values.dtype)], 0)


def short_masks(segment, length):
    masks = []
    for offset in range(SHORT):
        earlier = jnp.concatenate([jnp.full((offset,), -1, jnp.int32), segment[: length - offset]])
        masks.append((earlier == segment).astype(jnp.float32)[:, None])
    return masks


def padded_rows(flat_values, row_count):
    total = flat_values.shape[0]
    row_width = -(-total // row_count)
    padded = jnp.concatenate(
        [flat_values, jnp.zeros((row_count * row_width - total,), flat_values.dtype)]
    )
    return padded.reshape(row_count, row_width)


def shards(feats, short_filter, medium_filter, doc_ids, counts, plan, cotangent):
    replicas = lax.axis_size("dp")
    zeros_count = lax.axis_size("zero")
    tile_count = replicas * zeros_count
    length = feats.shape[0]
    width = cotangent.shape[1]
    member = (plan[0] == jnp.arange(replicas)).astype(jnp.float32)
    totals = lax.psum(member * counts[0].astype(jnp.float32), ("dp", "zero"))
    weighting = length * tile_count / (replicas * jnp.sum(member * totals))
    gathered = lax.all_gather(short_filter, "zero", axis=1, tiled=True)
    segment = doc_ids[0]
    masks = short_masks(segment, length)
    position = jnp.arange(length)
    living = (position < counts[0]).astype(jnp.float32)[:, None]
    convolved = jnp.zeros(feats.shape, jnp.float32)
    for offset in range(SHORT):
        convolved = (
            convolved
            + gathered[offset].astype(jnp.float32)
            * shift_down(feats, offset).astype(jnp.float32)
            * masks[offset]
        )
    query_part = convolved[:, :width]
    key_part = convolved[:, width : 2 * width]
    value_part = convolved[:, 2 * width :]
    product = (key_part * value_part).astype(jnp.bfloat16)
    groups = medium_filter.shape[1]
    taps_count = medium_filter.shape[0]
    gsize_here = width // groups
    product_cols = product.reshape(length, groups, gsize_here).transpose(1, 2, 0)
    lag_index = jnp.arange(taps_count)[:, None, None]
    later = position[None, :, None]
    earlier = position[None, None, :]
    same_doc = (segment[:, None] == segment[None, :])[None]
    selector = (
        ((later - earlier == lag_index) & same_doc)
        .astype(jnp.bfloat16)
        .reshape(taps_count, length * length)
    )
    taps_rows = medium_filter.astype(jnp.bfloat16).T
    toeplitz = jnp.dot(taps_rows, selector, preferred_element_type=jnp.float32).astype(jnp.bfloat16)
    toeplitz = toeplitz.reshape(groups, length, length)
    long_cols = jnp.einsum(
        "gts,gcs->gct", toeplitz, product_cols, preferred_element_type=jnp.float32
    )
    long_conv = long_cols.transpose(2, 0, 1).reshape(length, width)
    mixed = (living * query_part * long_conv).astype(jnp.bfloat16)
    grad_out = cotangent.astype(jnp.float32) * living * weighting
    grad_query = grad_out * long_conv
    grad_long = (grad_out * query_part).astype(jnp.bfloat16)
    grad_cols = grad_long.reshape(length, groups, gsize_here).transpose(1, 2, 0)
    grad_prod_cols = jnp.einsum(
        "gts,gct->gcs", toeplitz, grad_cols, preferred_element_type=jnp.float32
    )
    grad_product = grad_prod_cols.transpose(2, 0, 1).reshape(length, width)
    crossed = jnp.einsum(
        "gct,gcs->gts", grad_cols, product_cols, preferred_element_type=jnp.float32
    )
    crossed = crossed.reshape(groups, length * length)
    medium_part = lax.dot_general(
        crossed,
        selector.astype(jnp.float32),
        (((1,), (1,)), ((), ())),
        precision=lax.Precision.HIGHEST,
    ).T
    grad_short = jnp.concatenate(
        [grad_query, grad_product * value_part, grad_product * key_part], 1
    )
    grad_feats = jnp.zeros(feats.shape, jnp.float32)
    short_rows = []
    for offset in range(SHORT):
        masked = grad_short * masks[offset]
        grad_feats = grad_feats + gathered[offset].astype(jnp.float32) * shift_up(masked, offset)
        short_rows.append(jnp.sum(masked * shift_down(feats, offset).astype(jnp.float32), 0))
    short_local = jnp.stack(short_rows)
    medium_total = taps_count * groups
    slice_width = short_local.shape[1] // zeros_count
    short_part = short_local.reshape(SHORT, zeros_count, slice_width)
    short_part = short_part.transpose(1, 0, 2).reshape(zeros_count, SHORT * slice_width)
    medium_rows = padded_rows(medium_part.reshape(medium_total), zeros_count)
    joined = jnp.concatenate([short_part, medium_rows], 1)
    own_share = lax.psum_scatter(joined, "zero", scatter_dimension=0, tiled=True)
    own_share = lax.psum(own_share, "dp")
    short_grad = own_share[0, : SHORT * slice_width].reshape(SHORT, slice_width)
    medium_all = lax.all_gather(own_share[:, SHORT * slice_width :], "zero", axis=0, tiled=True)
    medium_grad = medium_all.reshape(-1)[:medium_total].reshape(taps_count, groups)
    return (mixed, grad_feats.astype(jnp.bfloat16), short_grad, medium_grad)


def solution(mesh):
    in_specs = (
        P(("dp", "zero"), None),
        P(None, "zero"),
        P(),
        P(("dp", "zero"), None),
        P(("dp", "zero")),
        P(("dp", "zero")),
        P(("dp", "zero"), None),
    )
    out_specs = (P(("dp", "zero"), None), P(("dp", "zero"), None), P(None, "zero"), P())
    return jax.shard_map(shards, mesh=mesh, in_specs=in_specs, out_specs=out_specs, check_vma=False)
```

profile of v0, /device:TPU:0, one launch (start us, length us, event | category | flops | bytes accessed | tf_op | source)
XLA Modules:
  0.0 236.5 jit_solution(1782118033775709187)
XLA Ops:
  12.5 42.0 %psum.14 = f32[4]{0:T(128)S(1)} all-reduce(f32[4]{0:T(128)S(1)} %compare_select_fusion.1), channel_id=1, replica_groups=mesh['dp'=4,'zero'=8] {'dp','zero'}, use_global_device_ids=true, to_apply=%region_0.0 | all-reduce | flops 4 | bytes 32 | tf_op jit(solution)/shard_map/psum | solution.py:43
  56.9 14.1 %all_gather.6 = bf16[7,6144]{1,0:T(8,128)(2,1)S(1)} all-gather(bf16[7,768]{1,0:T(8,128)(2,1)} %param.8), channel_id=1, replica_groups=mesh['dp'=4,'zero'=8] {'zero'}, dimensions={1}, use_global_device_ids=true | all-gather | bytes 96768 | tf_op jit(solution)/shard_map/all_gather | solution.py:45
  71.2 2.0 copy.39
  73.2 1.9 copy.31
  75.2 8.6 %fusion.15 = f32[128,6144]{0,1:T(8,128)S(1)} fusion(bf16[128,6144]{0,1:T(8,128)(2,1)S(1)} %copy.31, f32[128]{0:T(128)S(1)} %get-tuple-element.50, f32[6144]{0:T(1024)S(1)} %bitcast.101, f32[128]{0:T(128)S(1)} %get-tuple-element.49, f32[6144]{0:T(1024)S(1)} %bitcast.103, f32[128]{0:T(128)S(1)} %get-tuple-element.48, f32[6144]{0:T(1024)S(1)} %bitcast.105, ...), kind=kLoop, calls=%fused_computation.30 | loop fusion | flops 20447232 | bytes 14072832 | tf_op jit(solution)/shard_map/add | solution.py:53
  83.8 1.7 copy-done.1
  85.7 4.3 %convolution_convert_fusion = bf16[16384,128]{1,0:T(8,128)(2,1)} fusion(s32[16384]{0:T(1024)S(1)} %fusion.36, pred[16384]{0:T(1024)(128)(4,1)S(1)} %bitcast_compare_fusion, f32[128,128]{1,0:T(8,128)S(1)} %copy-done.14), kind=kOutput, calls=%fused_computation | convolution fusion | flops 543178752 | bytes 4341760 | tf_op jit(solution)/shard_map/dot_general | solution.py:76
  90.0 6.6 %copy.38 = bf16[128,128,128]{2,1,0:T(8,128)(2,1)} copy(bf16[128,128,128]{0,2,1:T(8,128)(2,1)} %bitcast.95) | data formatting | bytes 8388608 | tf_op jit(solution)/shard_map/reshape | solution.py:77
  98.0 4.6 %fusion.38 = f32[128,16,128]{2,1,0:T(8,128)S(1)} fusion(bf16[128,16,128]{2,1,0:T(8,128)(2,1)S(1)} %bitcast.91, bf16[128,128,128]{2,1,0:T(8,128)(2,1)} %copy.38), kind=kOutput, calls=%fused_computation.100 | convolution fusion | flops 67108864 | bytes 5767168 | tf_op jit(solution)/shard_map/gts,gcs->gct/dot_general | solution.py:78
  102.6 2.3 multiply_convert_fusion
  105.0 1.2 fusion.39
  106.2 4.5 %fusion.40 = f32[128,128,128]{2,1,0:T(8,128)} fusion(bf16[128,16,128]{2,1,0:T(8,128)(2,1)S(1)} %bitcast.94, bf16[128,16,128]{2,1,0:T(8,128)(2,1)S(1)} %bitcast.92), kind=kOutput, calls=%fused_computation.102 | convolution fusion | flops 67108864 | bytes 9437184 | tf_op jit(solution)/shard_map/gct,gcs->gts/dot_general | solution.py:91
  111.0 8.4 %fusion.24 = (f32[6144]{0:T(1024)S(1)}, f32[128,6144]{0,1:T(8,128)}, f32[6144]{0:T(1024)S(1)}, f32[128,6144]{0,1:T(8,128)}, f32[6144]{0:T(1024)S(1)}, /*index=5*/f32[128,6144]{0,1:T(8,128)}) fusion(bf16[124,6144]{0,1:T(8,128)(2,1)S(1)} %bitcast.87, f32[128]{0:T(128)S(1)} %get-tuple-element.48, f32[128,2048]{0,1:T(8,128)S(1)} %get-tuple-element.25, ...), kind=kLoop, calls=%fused_computation.39 | loop fusion | flops 10991616 | bytes 17192448 | tf_op jit(solution)/shard_map/reduce_sum | solution.py:109
  119.4 9.5 %fusion.18 = (f32[6144]{0:T(1024)S(1)}, f32[128,6144]{0,1:T(8,128)}, f32[6144]{0:T(1024)S(1)}, f32[6144]{0:T(1024)S(1)}, f32[128,6144]{0,1:T(8,128)}, /*index=5*/f32[6144]{0:T(1024)S(1)}, f32[128,6144]{0,1:T(8,128)}) fusion(bf16[127,6144]{0,1:T(8,128)(2,1)S(1)} %bitcast.90, f32[128]{0:T(128)S(1)} %get-tuple-element.45, ...), kind=kLoop, calls=%fused_computation.33 | loop fusion | flops 13344768 | bytes 18900480 | tf_op jit(solution)/shard_map/reduce_sum | solution.py:109
  129.0 12.7 %fusion.29 = f32[128,128]{1,0:T(8,128)S(1)} fusion(f32[128,128,128]{2,1,0:T(8,128)} %fusion.40, s32[128,128]{1,0:T(8,128)S(1)} %iota_subtract_fusion, pred[128,128]{1,0:T(8,128)(4,1)S(1)} %broadcast_compare_fusion), kind=kOutput, calls=%fused_computation.52 | convolution fusion | flops 3225419776 | bytes 8536064 | tf_op jit(solution)/shard_map/dot_general | solution.py:95
  142.6 2.9 %slice.173 = f32[124,6144]{0,1:T(8,128)S(1)} slice(f32[128,6144]{0,1:T(8,128)} %get-tuple-element.17), slice={[4:128], [0:6144]} | slice | bytes 6094848 | tf_op jit(solution)/shard_map/slice | solution.py:16
  148.3 1.0 copy-done.11
  152.1 1.0 copy-done.9
  154.6 9.5 %add_convert_fusion = bf16[128,6144]{0,1:T(8,128)(2,1)S(1)} fusion(f32[122,6144]{0,1:T(8,128)S(1)} %slice.175, f32[123,6144]{0,1:T(8,128)S(1)} %slice.174, f32[124,6144]{0,1:T(8,128)S(1)} %slice.173, f32[125,6144]{0,1:T(8,128)S(1)} %slice.172, f32[126,6144]{0,1:T(8,128)S(1)} %slice.171, f32[127,6144]{0,1:T(8,128)S(1)} %slice.170, f32[6144]{0:T(1024)S(1)} %bitcast.102, ...), kind=kLoop, calls=%fused_computation.45 | loop fusion | flops 12582912 | bytes 23248896 | tf_op jit(solution)/shard_map/convert_element_type | solution.py:122
  165.2 1.6 copy.43
  167.3 27.7 %all-reduce.20.cloned.1.call-done = f32[8,7424]{1,0:T(8,128)} async-done(((f32[8,7424]{1,0:T(8,128)}), f32[8,7424]{1,0:T(8,128)}) %all-reduce.20.cloned.1.call-update) | async-done | bytes 237584
  195.1 1.6 constant_dynamic-slice_fusion
  196.7 16.3 %psum.15 = f32[1,7424]{1,0:T(1,128)S(1)} all-reduce(f32[1,7424]{1,0:T(1,128)S(1)} %constant_dynamic-slice_fusion), channel_id=1, replica_groups=mesh['dp'=4,'zero'=8] {'dp'}, use_global_device_ids=true, to_apply=%region_10.0 | all-reduce | flops 7424 | bytes 59392 | tf_op jit(solution)/shard_map/psum | solution.py:118
  213.7 15.3 %all-gather = f32[8,1,2048]{2,1,0:T(1,128)S(1)} all-gather(f32[1,1,2048]{2,1,0:T(1,128)S(1)} %slice_bitcast_fusion), channel_id=1, replica_groups=mesh['dp'=4,'zero'=8] {'zero'}, dimensions={0}, use_global_device_ids=true | all-gather | bytes 73728 | tf_op jit(solution)/shard_map/all_gather | solution.py:120
  (76 shorter events, 18.4 us)
Async XLA Ops:
  7.2 67.9 %copy-start.13 = (s32[1,128]{1,0:T(1,128)S(1)}, s32[1,128]{1,0:T(1,128)}, u32[]{:S(2)}) copy-start(s32[1,128]{1,0:T(1,128)} %param.10) | copy-start | bytes 1540
  7.2 187.9 %all-reduce.20.cloned.1.call-start = ((), (), s32[]{:S(2)}) async-start(), calls=%async_computation | async-start | bytes 475136
  75.2 10.5 %copy-start.14 = (f32[128,128]{1,0:T(8,128)S(1)}, f32[128,128]{1,0:T(8,128)}, u32[]{:S(2)}) copy-start(f32[128,128]{1,0:T(8,128)} %param.9) | copy-start | bytes 196612
  83.8 1.8 copy-start.1
  98.0 4.6 %copy-start.2 = (f32[128,6144]{0,1:T(8,128)S(1)}, f32[128,6144]{0,1:T(8,128)}, u32[]{:S(2)}) copy-start(f32[128,6144]{0,1:T(8,128)} %copy-done.1) | copy-start | bytes 9437188
  102.6 2.4 %copy-start = (bf16[128,128,128]{2,1,0:T(8,128)(2,1)S(1)}, bf16[128,128,128]{2,1,0:T(8,128)(2,1)}, u32[]{:S(2)}) copy-start(bf16[128,128,128]{2,1,0:T(8,128)(2,1)} %copy.38) | copy-start | bytes 12582916
  111.0 8.4 %copy-start.3 = (f32[128,2048]{0,1:T(8,128)}, f32[128,2048]{0,1:T(8,128)S(1)}, u32[]{:S(2)}) copy-start(f32[128,2048]{0,1:T(8,128)S(1)} %get-tuple-element.24) | copy-start | bytes 3145732
  111.0 8.4 %copy-start.5 = (f32[128,2048]{0,1:T(8,128)}, f32[128,2048]{0,1:T(8,128)S(1)}, u32[]{:S(2)}) copy-start(f32[128,2048]{0,1:T(8,128)S(1)} %get-tuple-element.25) | copy-start | bytes 3145732
  142.6 2.9 %copy-start.8 = (f32[128,6144]{0,1:T(8,128)S(1)}, f32[128,6144]{0,1:T(8,128)}, u32[]{:S(2)}) copy-start(f32[128,6144]{0,1:T(8,128)} %get-tuple-element.34) | copy-start | bytes 9437188
  145.5 1.9 copy-start.7
  147.4 1.9 copy-start.11
  149.3 1.9 copy-start.10
  151.2 1.9 copy-start.9
  153.1 1.2 copy-start.4
  153.1 1.5 copy-start.6
  154.6 9.5 %copy-start.12 = (bf16[128,2048]{0,1:T(8,128)(2,1)S(1)}, bf16[128,2048]{0,1:T(8,128)(2,1)}, u32[]{:S(2)}) copy-start(bf16[128,2048]{0,1:T(8,128)(2,1)} %get-tuple-element.27) | copy-start | bytes 1572868
  164.2 2.6 %copy-start.15 = (u32[32]{0:T(128)S(1)}, u32[32]{0:T(128)}, u32[]{:S(2)}) copy-start(u32[32]{0:T(128)} %constant.70) | copy-start | bytes 388
Sparse Core Ops, SparseCore 0:
  142.7 52.3 all-reduce.19
where the time goes:
time: 237 us; the launch traced here: 236 us
  blocking collectives  87.8 us (37%)
  other arithmetic  41.8 us (18%)
  local copies, waits for them, and re-layouts  35.4 us (15%)
  waiting for transfers between devices  27.7 us (12%)
  matrix products  27.4 us (12%)
  between operations  16.4 us (7%)
    psum x1, blocking collectives, shards(): totals = lax.psum(member * counts[0].astype(jnp.float32), ('dp', 'zero'))  42 us
    unnamed x2, waiting for transfers between devices  27.7 us
    reduce_sum x2, other arithmetic, shards(): jnp.sum(masked * shift_down(feats, offset).astype(jnp.float32), 0)  17.9 us
    psum x1, blocking collectives, shards(): own_share = lax.psum(own_share, 'dp')  16.3 us
    unnamed x46, local copies, waits for them, and re-layouts  15.9 us
    all_gather x1, blocking collectives, shards(): lax.all_gather(own_share[:, SHORT * slice_width:], 'zero', axis=0, tiled=...  15.3 us
    all_gather x1, blocking collectives, shards(): gathered = lax.all_gather(short_filter, 'zero', axis=1, tiled=True)  14.1 us
    dot_general x1, matrix products, shards(): lax.dot_general(crossed, selector.astype(jnp.float32), (((1,), (1,)), (()...  12.7 us
  transfers between devices with their start and end apart: 1, of which 1 were waited for; matrix products, arithmetic and copies ran while one was open for 8% of the time, Pallas kernels for 0%

commit v1 on v0

v1 whole, which is shorter than its diff:
```python
import functools

import jax
import jax.numpy as jnp
from jax import lax
from jax.experimental import pallas as pl
from jax.experimental.pallas import tpu as pltpu
from jax.sharding import PartitionSpec as P

F32 = jnp.float32
BF16 = jnp.bfloat16
MESH = pl.DeviceIdType.MESH
LANES = 128
WIDE = 256


def greet(replicas, zeros):
    barrier = pltpu.get_barrier_semaphore()
    mine, row = lax.axis_index("zero"), lax.axis_index("dp")
    for step in range(1, zeros):
        peer = lax.rem(mine + step, zeros)
        pl.semaphore_signal(barrier, inc=1, device_id={"zero": peer}, device_id_type=MESH)
    for step in range(1, replicas):
        peer = lax.rem(row + step, replicas)
        pl.semaphore_signal(barrier, inc=1, device_id={"dp": peer}, device_id_type=MESH)
    return barrier


def spread(axis, count, source, slots, send, recv):
    me = lax.axis_index(axis)
    copies = []
    for step in range(1, count):
        peer = lax.rem(me + step, count)
        copy = pltpu.make_async_remote_copy(
            src_ref=source(peer),
            dst_ref=slots.at[me],
            send_sem=send.at[step],
            recv_sem=recv.at[step],
            device_id={axis: peer},
            device_id_type=MESH,
        )
        copy.start()
        copies.append(copy)
    return copies


def gather_kernel(
    replicas, zeros, scale, short, filt, counts, plan, filters, weight,
    rows, stage, slots, tally, tallies, send, recv, tsend, trecv,
):
    barrier = greet(replicas, zeros)
    mine, row = lax.axis_index("zero"), lax.axis_index("dp")
    cw = filt.shape[1]
    half = cw // 2
    lane = lax.broadcasted_iota(jnp.int32, (1, cw), 1)
    rows[0:short, :] = filt[...].astype(F32)
    rows[short:8, :] = jnp.where(lane == plan[0], counts[0].astype(F32), 0.0)
    stage[...] = jnp.concatenate([rows[:, :half], rows[:, half:]], 0).astype(BF16)
    slots[mine] = stage[...]
    pl.semaphore_wait(barrier, zeros + replicas - 2)
    copies = spread("zero", zeros, lambda peer: stage, slots, send, recv)
    for copy in copies:
        copy.wait()
    total = slots[0].astype(F32)[short : short + 1, :LANES]
    for z in range(1, zeros):
        total = total + slots[z].astype(F32)[short : short + 1, :LANES]
    tally[...] = jnp.broadcast_to(total, (8, LANES))
    tallies[row] = tally[...]
    copies = spread("dp", replicas, lambda peer: tally, tallies, tsend, trecv)
    for z in range(zeros):
        block = slots[z].astype(F32)
        filters[:, z * cw : z * cw + half] = block[0:8]
        filters[:, z * cw + half : (z + 1) * cw] = block[8:16]
    for copy in copies:
        copy.wait()
    total = tallies[0]
    for r in range(1, replicas):
        total = total + tallies[r]
    lane8 = lax.broadcasted_iota(jnp.int32, (8, LANES), 1)
    own = jnp.sum(jnp.where(lane8 == plan[0], total, 0.0), 1, keepdims=True)
    weight[...] = jnp.broadcast_to(scale / own, (8, LANES))


def reduce_kernel(
    replicas, zeros, short, shorts, medium, short_out, medium_out,
    pack, slots, part, parts, share, shares, send, recv, psend, precv, msend, mrecv,
):
    barrier = greet(replicas, zeros)
    mine, row = lax.axis_index("zero"), lax.axis_index("dp")
    cw = shorts.shape[1] // zeros
    half = cw // 2
    depth = medium.shape[0] // zeros
    for z in range(zeros):
        one = shorts[:, z * cw : z * cw + half]
        two = shorts[:, z * cw + half : (z + 1) * cw]
        pack[z, :, :half] = jnp.concatenate([one, two], 0).astype(BF16)
        pack[z, :, half:] = medium[z * depth : (z + 1) * depth, :].astype(BF16)
    slots[mine] = pack[mine]
    pl.semaphore_wait(barrier, zeros + replicas - 2)
    copies = spread("zero", zeros, lambda peer: pack.at[peer], slots, send, recv)
    for copy in copies:
        copy.wait()
    total = slots[0].astype(F32)
    for z in range(1, zeros):
        total = total + slots[z].astype(F32)
    part[...] = total
    parts[row] = total
    copies = spread("dp", replicas, lambda peer: part, parts, psend, precv)
    for copy in copies:
        copy.wait()
    total = parts[0]
    for r in range(1, replicas):
        total = total + parts[r]
    share[...] = total[:, half:]
    shares[mine] = total[:, half:]
    copies = spread("zero", zeros, lambda peer: share, shares, msend, mrecv)
    short_out[:, :half] = total[0:short, :half]
    short_out[:, half:] = total[8 : 8 + short, :half]
    for copy in copies:
        copy.wait()
    for z in range(zeros):
        medium_out[z * depth : (z + 1) * depth, :] = shares[z]


def dot(a, b):
    return jnp.dot(a, b, preferred_element_type=F32)


def block_kernel(
    short, gsize, counts, doc, taps, weight, cot, fq, fk, fv, wq, wk, wv,
    mixed, grads, shorts, medium,
    down, up, causal, causal_t, causal_r, flip, tap_rows, tap_back, living, med,
):
    step = pl.program_id(0)
    length = cot.shape[0]
    width = grads.shape[1] // 3
    per = LANES // gsize
    square = (length, length)

    @pl.when(step == 0)
    def _():
        r = lax.broadcasted_iota(jnp.int32, square, 0)
        c = lax.broadcasted_iota(jnp.int32, square, 1)
        across = jnp.broadcast_to(doc[...].astype(F32), square)
        same = (across == across.T).astype(F32)
        for j in range(short):
            down[j] = jnp.where(r - c == j, same, 0.0).astype(BF16)
            up[j] = jnp.where(c - r == j, same, 0.0).astype(BF16)
        low = jnp.where(r >= c, same, 0.0)
        causal[...] = low
        causal_t[...] = jnp.where(c >= r, same, 0.0)
        turned = (r + c == length - 1).astype(BF16)
        flip[...] = turned
        causal_r[...] = dot(low.astype(BF16), turned)
        rounded = taps[...].astype(BF16).astype(F32).T
        tap_rows[...] = rounded
        back = (lax.rem(r + c, length) == 0).astype(BF16)
        tap_back[...] = dot(rounded.astype(BF16), back)
        living[...] = (r < counts[0]).astype(F32)

    def convolve(feats, filt):
        x = feats[...]
        total = filt[0:1, :] * x.astype(F32)
        for j in range(1, short):
            total = total + filt[j : j + 1, :] * dot(down[j], x)
        return total

    query, key, value = convolve(fq, wq), convolve(fk, wk), convolve(fv, wv)
    lane = lax.broadcasted_iota(jnp.int32, (1, LANES), 1)
    picks = [(lane // gsize == i).astype(BF16) for i in range(per)]
    weighting = weight[0:1, :]
    pieces = [[], [], []]
    for h in range(cot.shape[1] // LANES):
        cols = slice(h * LANES, (h + 1) * LANES)
        q, k, v = query[:, cols], key[:, cols], value[:, cols]
        product = (k * v).astype(BF16)
        first = step * (cot.shape[1] // gsize) + h * per
        forward, backward = [], []
        for i in range(per):
            row = jnp.broadcast_to(tap_back[pl.ds(first + i, 1), :], square)
            row = pltpu.roll(row, 0, 1, stride=1, stride_axis=0)
            forward.append((row * causal[...]).astype(BF16))
            row = jnp.broadcast_to(tap_rows[pl.ds(first + i, 1), :], square)
            row = pltpu.roll(row, 0, 1, stride=1, stride_axis=0)
            backward.append((row * causal_t[...]).astype(BF16))
        long_conv = dot(
            jnp.concatenate(forward, 1), jnp.concatenate([product * m for m in picks], 0)
        )
        alive = living[...]
        mixed[:, cols] = (alive * q * long_conv).astype(BF16)
        grad_out = cot[:, cols].astype(F32) * alive * weighting
        grad_long = (grad_out * q).astype(BF16)
        chosen = jnp.concatenate([grad_long * m for m in picks], 0)
        grad_product = dot(jnp.concatenate(backward, 1), chosen)
        turned = dot(flip[...], product).astype(BF16)
        crossed = lax.dot_general(
            chosen, turned, (((1,), (1,)), ((), ())), preferred_element_type=F32
        )
        for i in range(per):
            part = crossed[i * length : (i + 1) * length] * causal_r[...]
            part = pltpu.roll(part, 1, 1, stride=1, stride_axis=0)
            med[pl.ds(first + i, 1), :] = jnp.sum(part, 0, keepdims=True)
        pieces[0].append((grad_out * long_conv).astype(BF16))
        pieces[1].append((grad_product * v).astype(BF16))
        pieces[2].append((grad_product * k).astype(BF16))

    span = cot.shape[1]
    for n, (feats, filt) in enumerate(((fq, wq), (fk, wk), (fv, wv))):
        grad = jnp.concatenate(pieces[n], 1)
        x = feats[...].astype(F32)
        where = pl.ds(pl.multiple_of(n * width + step * span, LANES), span)
        total = None
        for j in range(short):
            moved = grad.astype(F32) if j == 0 else dot(up[j], grad)
            term = filt[j : j + 1, :] * moved
            total = term if total is None else total + term
            shorts[j : j + 1, where] = jnp.sum(moved * x, 0, keepdims=True)
        shorts[short:8, where] = jnp.zeros((8 - short, span), F32)
        grads[:, where] = total.astype(BF16)

    @pl.when(step == pl.num_programs(0) - 1)
    def _():
        medium[...] = med[...].T


def run_block(feats, filters, medium_filter, doc_ids, counts, weight, cotangent, short):
    length, width = cotangent.shape
    taps_count, groups = medium_filter.shape
    steps = width // WIDE
    square = (length, length)

    def part(n):
        return pl.BlockSpec((length, WIDE), lambda i, n=n: (0, n * steps + i))

    def part8(n):
        return pl.BlockSpec((8, WIDE), lambda i, n=n: (0, n * steps + i))

    def whole(shape):
        return pl.BlockSpec(shape, lambda i: (0, 0))

    return pl.pallas_call(
        functools.partial(block_kernel, short, width // groups),
        grid=(steps,),
        in_specs=[
            pl.BlockSpec(memory_space=pltpu.SMEM),
            whole((1, length)),
            whole((taps_count, groups)),
            whole((8, LANES)),
            part(0), part(0), part(1), part(2), part8(0), part8(1), part8(2),
        ],
        out_specs=[part(0), whole(feats.shape), whole((8, 3 * width)), whole((taps_count, groups))],
        out_shape=[
            jax.ShapeDtypeStruct((length, width), BF16),
            jax.ShapeDtypeStruct(feats.shape, BF16),
            jax.ShapeDtypeStruct((8, 3 * width), F32),
            jax.ShapeDtypeStruct((taps_count, groups), F32),
        ],
        scratch_shapes=[
            pltpu.VMEM((short, length, length), BF16),
            pltpu.VMEM((short, length, length), BF16),
            pltpu.VMEM(square, F32),
            pltpu.VMEM(square, F32),
            pltpu.VMEM(square, F32),
            pltpu.VMEM(square, BF16),
            pltpu.VMEM((groups, taps_count), F32),
            pltpu.VMEM((groups, taps_count), F32),
            pltpu.VMEM((length, LANES), F32),
            pltpu.VMEM((groups, taps_count), F32),
        ],
        compiler_params=pltpu.CompilerParams(vmem_limit_bytes=40 * 1024 * 1024),
        name="conv_block",
    )(counts, doc_ids, medium_filter, weight, cotangent, feats, feats, feats, filters, filters, filters)


def vmem(count):
    return [pl.BlockSpec(memory_space=pltpu.VMEM)] * count


def run_gather(short_filter, counts, plan, replicas, zeros, scale):
    short, cw = short_filter.shape
    half = cw // 2
    return pl.pallas_call(
        functools.partial(gather_kernel, replicas, zeros, scale, short),
        in_specs=vmem(1) + [pl.BlockSpec(memory_space=pltpu.SMEM)] * 2,
        out_specs=vmem(2),
        out_shape=[
            jax.ShapeDtypeStruct((8, cw * zeros), F32),
            jax.ShapeDtypeStruct((8, LANES), F32),
        ],
        scratch_shapes=[
            pltpu.VMEM((8, cw), F32),
            pltpu.VMEM((16, half), BF16),
            pltpu.VMEM((zeros, 16, half), BF16),
            pltpu.VMEM((8, LANES), F32),
            pltpu.VMEM((replicas, 8, LANES), F32),
            pltpu.SemaphoreType.DMA((zeros,)),
            pltpu.SemaphoreType.DMA((zeros,)),
            pltpu.SemaphoreType.DMA((replicas,)),
            pltpu.SemaphoreType.DMA((replicas,)),
        ],
        compiler_params=pltpu.CompilerParams(collective_id=0, has_side_effects=True),
        name="gather_filters",
    )(short_filter, counts, plan)


def run_reduce(shorts, medium, replicas, zeros, short):
    cw = shorts.shape[1] // zeros
    half = cw // 2
    taps_count, groups = medium.shape
    depth = taps_count // zeros
    return pl.pallas_call(
        functools.partial(reduce_kernel, replicas, zeros, short),
        in_specs=vmem(2),
        out_specs=vmem(2),
        out_shape=[
            jax.ShapeDtypeStruct((short, cw), F32),
            jax.ShapeDtypeStruct((taps_count, groups), F32),
        ],
        scratch_shapes=[
            pltpu.VMEM((zeros, 16, half + groups), BF16),
            pltpu.VMEM((zeros, 16, half + groups), BF16),
            pltpu.VMEM((16, half + groups), F32),
            pltpu.VMEM((replicas, 16, half + groups), F32),
            pltpu.VMEM((depth, groups), F32),
            pltpu.VMEM((zeros, depth, groups), F32),
            pltpu.SemaphoreType.DMA((zeros,)),
            pltpu.SemaphoreType.DMA((zeros,)),
            pltpu.SemaphoreType.DMA((replicas,)),
            pltpu.SemaphoreType.DMA((replicas,)),
            pltpu.SemaphoreType.DMA((zeros,)),
            pltpu.SemaphoreType.DMA((zeros,)),
        ],
        compiler_params=pltpu.CompilerParams(collective_id=1, has_side_effects=True),
        name="reduce_filters",
    )(shorts, medium)


def shards(feats, short_filter, medium_filter, doc_ids, counts, plan, cotangent):
    replicas = lax.axis_size("dp")
    zeros = lax.axis_size("zero")
    length = feats.shape[0]
    short, cw = short_filter.shape
    scale = float(length * replicas * zeros / replicas)
    packed = cw % WIDE == 0 and medium_filter.shape[0] == 16 * zeros
    if packed:
        filters, weight = run_gather(short_filter, counts, plan, replicas, zeros, scale)
    else:
        member = (plan[0] == jnp.arange(replicas)).astype(F32)
        totals = lax.psum(member * counts[0].astype(F32), ("dp", "zero"))
        weight = jnp.broadcast_to(scale / jnp.sum(member * totals), (8, LANES))
        filters = lax.all_gather(short_filter, "zero", axis=1, tiled=True).astype(F32)
        filters = jnp.pad(filters, ((0, 8 - short), (0, 0)))
    mixed, grads, shorts, medium = run_block(
        feats, filters, medium_filter, doc_ids, counts, weight, cotangent, short
    )
    if packed:
        short_grad, medium_grad = run_reduce(shorts, medium, replicas, zeros, short)
    else:
        own = lax.psum(shorts[:short], "dp")
        own = own.reshape(short, zeros, cw).transpose(1, 0, 2)
        short_grad = lax.psum_scatter(own, "zero", scatter_dimension=0, tiled=True)[0]
        medium_grad = lax.psum(medium, ("dp", "zero"))
    return mixed, grads, short_grad, medium_grad


def solution(mesh):
    in_specs = (
        P(("dp", "zero"), None),
        P(None, "zero"),
        P(),
        P(("dp", "zero"), None),
        P(("dp", "zero")),
        P(("dp", "zero")),
        P(("dp", "zero"), None),
    )
    out_specs = (P(("dp", "zero"), None), P(("dp", "zero"), None), P(None, "zero"), P())
    return jax.shard_map(shards, mesh=mesh, in_specs=in_specs, out_specs=out_specs, check_vma=False)
```

time: 237 us -> 58.3 us (0.25)
  blocking collectives: 87.8 us -> 0 us
  Pallas kernels: 0 us -> 46.2 us
  other arithmetic: 41.8 us -> 0 us
  waiting for transfers between devices: 27.7 us -> 0 us
  matrix products: 27.4 us -> 0 us
  local copies, waits for them, and re-layouts: 35.4 us -> 9.67 us
  between operations: 16.4 us -> 1.96 us
    psum x2 -> x0, blocking collectives: 58.4 us -> none  [the longest x1 42 us: shards(): totals = lax.psum(member * counts[0].astype(jnp.float32), ('dp', 'zero'))]
    pallas_call x0 -> x3, Pallas kernels: none -> 46.2 us  [the longest x1 16.7 us: run_reduce(): pl.pallas_call(functools.partial(reduce_kernel, replicas, zeros, short),...]
    all_gather x2 -> x0, blocking collectives: 29.4 us -> none  [the longest x1 15.3 us: shards(): lax.all_gather(own_share[:, SHORT * slice_width:], 'zero', axis=0, tiled=...]
    unnamed x2 -> x0, waiting for transfers between devices: 27.7 us -> none
    dot_general x5 -> x0, matrix products: 27.4 us -> none  [the longest x1 12.7 us: shards(): lax.dot_general(crossed, selector.astype(jnp.float32), (((1,), (1,)), (()...]
    reduce_sum x3 -> x0, other arithmetic: 18.5 us -> none  [the longest x2 17.9 us: shards(): jnp.sum(masked * shift_down(feats, offset).astype(jnp.float32), 0)]
    convert_element_type x5 -> x0, other arithmetic: 12 us -> none  [the longest x1 9.5 us: shards(): return (mixed, grad_feats.astype(jnp.bfloat16), short_grad, medium_grad)]
    slice x12 -> x0, local copies, waits for them, and re-layouts: 10.6 us -> none  [the longest x6 7.28 us: shift_up(): values[offset:]]
  transfers between devices with their start and end apart: 1 -> 0, of which waited for: 1 -> 0; matrix products, arithmetic and copies ran while one was open for 8% -> 0% of each run, Pallas kernels for 0% -> 0%
where the time goes in v1:
time: 58.3 us; the launch traced here: 57.8 us
  Pallas kernels  46.2 us (79%)
  local copies, waits for them, and re-layouts  9.67 us (17%)
  between operations  1.96 us (3%)
    pallas_call x1, Pallas kernels, run_reduce(): pl.pallas_call(functools.partial(reduce_kernel, replicas, zeros, short),...  16.7 us
    pallas_call x1, Pallas kernels, run_block(): pl.pallas_call(functools.partial(block_kernel, short, width // groups), g...  15.9 us
    pallas_call x1, Pallas kernels, run_gather(): pl.pallas_call(functools.partial(gather_kernel, replicas, zeros, scale, s...  13.6 us
    unnamed x18, local copies, waits for them, and re-layouts  9.67 us

profile of v1, /device:TPU:0, one launch (start us, length us, event | category | flops | bytes accessed | tf_op | source)
XLA Modules:
  0.0 57.8 jit_solution(2871821556562233444)
XLA Ops:
  1.9 13.6 %gather_filters.1 = (f32[8,6144]{1,0:T(8,128)}, f32[8,128]{1,0:T(8,128)}) custom-call(bf16[7,768]{1,0:T(8,128)(2,1)} %filt.1, s32[1]{0:T(128)S(6)} %copy.13.counts, s32[1]{0:T(128)S(6)} %copy.14.plan), custom_call_target="tpu_custom_call" | custom-call | tf_op jit(solution)/shard_map/gather_filters/pallas_call | solution.py:282
  15.5 0.0 copy-start
  15.5 1.4 %copy-done = bf16[128,6144]{1,0:T(8,128)(2,1)S(1)} copy-done((bf16[128,6144]{1,0:T(8,128)(2,1)S(1)}, bf16[128,6144]{1,0:T(8,128)(2,1)}, u32[]{:S(2)}) %copy-start) | copy-done | bytes 1572888
  16.9 0.0 copy-start.1
  16.9 0.9 %copy-done.1 = f32[8,6144]{1,0:T(8,128)S(1)} copy-done((f32[8,6144]{1,0:T(8,128)S(1)}, f32[8,6144]{1,0:T(8,128)}, u32[]{:S(2)}) %copy-start.1) | copy-done | bytes 196632
  17.9 0.0 copy-start.2
  17.9 1.0 %copy-done.2 = bf16[128,2048]{1,0:T(8,128)(2,1)S(1)} copy-done((bf16[128,2048]{1,0:T(8,128)(2,1)S(1)}, bf16[128,2048]{1,0:T(8,128)(2,1)}, u32[]{:S(2)}) %copy-start.2) | copy-done | bytes 524312
  18.9 0.0 copy-start.4
  18.9 0.8 %copy-done.4 = f32[128,128]{1,0:T(8,128)S(1)} copy-done((f32[128,128]{1,0:T(8,128)S(1)}, f32[128,128]{1,0:T(8,128)}, u32[]{:S(2)}) %copy-start.4) | copy-done | bytes 65560
  19.7 0.0 copy-start.6
  19.7 0.7 %copy-done.6 = f32[8,128]{1,0:T(8,128)S(1)} copy-done((f32[8,128]{1,0:T(8,128)S(1)}, f32[8,128]{1,0:T(8,128)}, u32[]{:S(2)}) %copy-start.6) | copy-done | bytes 4120
  20.4 0.0 copy-start.7
  20.4 0.7 %copy-done.7 = s32[1,128]{1,0:T(1,128)S(1)} copy-done((s32[1,128]{1,0:T(1,128)S(1)}, s32[1,128]{1,0:T(1,128)}, u32[]{:S(2)}) %copy-start.7) | copy-done | bytes 536
  21.1 15.9 %conv_block.1 = (bf16[128,2048]{1,0:T(8,128)(2,1)}, bf16[128,6144]{1,0:T(8,128)(2,1)}, f32[8,6144]{1,0:T(8,128)S(1)}, f32[128,128]{1,0:T(8,128)S(1)}) custom-call(s32[1]{0:T(128)S(6)} %copy.13.counts, s32[1,128]{1,0:T(1,128)S(1)} %copy-done.7, f32[128,128]{1,0:T(8,128)S(1)} %copy-done.4, f32[8,128]{1,0:T(8,128)S(1)} %copy-done.6, ...), custom_call_target="tpu_custom_call" | custom-call | tf_op jit(solution)/shard_map/conv_block/pallas_call | solution.py:241
  37.0 0.0 copy-start.3
  37.0 0.7 %copy-done.3 = f32[8,6144]{1,0:T(8,128)} copy-done((f32[8,6144]{1,0:T(8,128)}, f32[8,6144]{1,0:T(8,128)S(1)}, u32[]{:S(2)}) %copy-start.3) | copy-done | bytes 196632
  37.6 0.0 copy-start.5
  37.6 0.6 %copy-done.5 = f32[128,128]{1,0:T(8,128)} copy-done((f32[128,128]{1,0:T(8,128)}, f32[128,128]{1,0:T(8,128)S(1)}, u32[]{:S(2)}) %copy-start.5) | copy-done | bytes 65560
  38.3 16.7 %reduce_filters.1 = (f32[7,768]{1,0:T(8,128)}, f32[128,128]{1,0:T(8,128)}) custom-call(f32[8,6144]{1,0:T(8,128)} %copy-done.3, f32[128,128]{1,0:T(8,128)} %copy-done.5), custom_call_target="tpu_custom_call" | custom-call | tf_op jit(solution)/shard_map/reduce_filters/pallas_call | solution.py:311
  55.0 1.3 %copy.15 = f32[7,768]{1,0:T(8,128)} copy(f32[7,768]{1,0:T(8,128)} %get-tuple-element.26) | data formatting | bytes 43008
  56.3 1.5 %copy.16 = f32[128,128]{1,0:T(8,128)} copy(f32[128,128]{1,0:T(8,128)} %get-tuple-element.27) | data formatting | bytes 131072
Async XLA Ops:
  15.5 1.4 %copy-start = (bf16[128,6144]{1,0:T(8,128)(2,1)S(1)}, bf16[128,6144]{1,0:T(8,128)(2,1)}, u32[]{:S(2)}) copy-start(bf16[128,6144]{1,0:T(8,128)(2,1)} %fv.1) | copy-start | bytes 4718596
  16.9 0.9 %copy-start.1 = (f32[8,6144]{1,0:T(8,128)S(1)}, f32[8,6144]{1,0:T(8,128)}, u32[]{:S(2)}) copy-start(f32[8,6144]{1,0:T(8,128)} %get-tuple-element.13.wq.wk.wv) | copy-start | bytes 589828
  17.9 1.0 %copy-start.2 = (bf16[128,2048]{1,0:T(8,128)(2,1)S(1)}, bf16[128,2048]{1,0:T(8,128)(2,1)}, u32[]{:S(2)}) copy-start(bf16[128,2048]{1,0:T(8,128)(2,1)} %cot.1) | copy-start | bytes 1572868
  18.9 0.8 %copy-start.4 = (f32[128,128]{1,0:T(8,128)S(1)}, f32[128,128]{1,0:T(8,128)}, u32[]{:S(2)}) copy-start(f32[128,128]{1,0:T(8,128)} %taps.1) | copy-start | bytes 196612
  19.7 0.7 %copy-start.6 = (f32[8,128]{1,0:T(8,128)S(1)}, f32[8,128]{1,0:T(8,128)}, u32[]{:S(2)}) copy-start(f32[8,128]{1,0:T(8,128)} %get-tuple-element.12.weight) | copy-start | bytes 12292
  20.4 0.7 %copy-start.7 = (s32[1,128]{1,0:T(1,128)S(1)}, s32[1,128]{1,0:T(1,128)}, u32[]{:S(2)}) copy-start(s32[1,128]{1,0:T(1,128)} %doc.1) | copy-start | bytes 1540
  37.0 0.7 %copy-start.3 = (f32[8,6144]{1,0:T(8,128)}, f32[8,6144]{1,0:T(8,128)S(1)}, u32[]{:S(2)}) copy-start(f32[8,6144]{1,0:T(8,128)S(1)} %get-tuple-element.16.shorts) | copy-start | bytes 589828
  37.6 0.6 %copy-start.5 = (f32[128,128]{1,0:T(8,128)}, f32[128,128]{1,0:T(8,128)S(1)}, u32[]{:S(2)}) copy-start(f32[128,128]{1,0:T(8,128)S(1)} %get-tuple-element.17.medium) | copy-start | bytes 196612

commit v2 on v1

--- a/solution.py
+++ b/solution.py
@@ -42,84 +42,6 @@
         copy.start()
         copies.append(copy)
     return copies
-
-
-def gather_kernel(
-    replicas, zeros, scale, short, filt, counts, plan, filters, weight,
-    rows, stage, slots, tally, tallies, send, recv, tsend, trecv,
-):
-    barrier = greet(replicas, zeros)
-    mine, row = lax.axis_index("zero"), lax.axis_index("dp")
-    cw = filt.shape[1]
-    half = cw // 2
-    lane = lax.broadcasted_iota(jnp.int32, (1, cw), 1)
-    rows[0:short, :] = filt[...].astype(F32)
-    rows[short:8, :] = jnp.where(lane == plan[0], counts[0].astype(F32), 0.0)
-    stage[...] = jnp.concatenate([rows[:, :half], rows[:, half:]], 0).astype(BF16)
-    slots[mine] = stage[...]
-    pl.semaphore_wait(barrier, zeros + replicas - 2)
-    copies = spread("zero", zeros, lambda peer: stage, slots, send, recv)
-    for copy in copies:
-        copy.wait()
-    total = slots[0].astype(F32)[short : short + 1, :LANES]
-    for z in range(1, zeros):
-        total = total + slots[z].astype(F32)[short : short + 1, :LANES]
-    tally[...] = jnp.broadcast_to(total, (8, LANES))
-    tallies[row] = tally[...]
-    copies = spread("dp", replicas, lambda peer: tally, tallies, tsend, trecv)
-    for z in range(zeros):
-        block = slots[z].astype(F32)
-        filters[:, z * cw : z * cw + half] = block[0:8]
-        filters[:, z * cw + half : (z + 1) * cw] = block[8:16]
-    for copy in copies:
-        copy.wait()
-    total = tallies[0]
-    for r in range(1, replicas):
-        total = total + tallies[r]
-    lane8 = lax.broadcasted_iota(jnp.int32, (8, LANES), 1)
-    own = jnp.sum(jnp.where(lane8 == plan[0], total, 0.0), 1, keepdims=True)
-    weight[...] = jnp.broadcast_to(scale / own, (8, LANES))
-
-
-def reduce_kernel(
-    replicas, zeros, short, shorts, medium, short_out, medium_out,
-    pack, slots, part, parts, share, shares, send, recv, psend, precv, msend, mrecv,
-):
-    barrier = greet(replicas, zeros)
-    mine, row = lax.axis_index("zero"), lax.axis_index("dp")
-    cw = shorts.shape[1] // zeros
-    half = cw // 2
-    depth = medium.shape[0] // zeros
-    for z in range(zeros):
-        one = shorts[:, z * cw : z * cw + half]
-        two = shorts[:, z * cw + half : (z + 1) * cw]
-        pack[z, :, :half] = jnp.concatenate([one, two], 0).astype(BF16)
-        pack[z, :, half:] = medium[z * depth : (z + 1) * depth, :].astype(BF16)
-    slots[mine] = pack[mine]
-    pl.semaphore_wait(barrier, zeros + replicas - 2)
-    copies = spread("zero", zeros, lambda peer: pack.at[peer], slots, send, recv)
-    for copy in copies:
-        copy.wait()
-    total = slots[0].astype(F32)
-    for z in range(1, zeros):
-        total = total + slots[z].astype(F32)
-    part[...] = total
-    parts[row] = total
-    copies = spread("dp", replicas, lambda peer: part, parts, psend, precv)
-    for copy in copies:
-        copy.wait()
-    total = parts[0]
-    for r in range(1, replicas):
-        total = total + parts[r]
-    share[...] = total[:, half:]
-    shares[mine] = total[:, half:]
-    copies = spread("zero", zeros, lambda peer: share, shares, msend, mrecv)
-    short_out[:, :half] = total[0:short, :half]
-    short_out[:, half:] = total[8 : 8 + short, :half]
-    for copy in copies:
-        copy.wait()
-    for z in range(zeros):
-        medium_out[z * depth : (z + 1) * depth, :] = shares[z]
 
 
 def dot(a, b):
@@ -272,67 +194,330 @@
     )(counts, doc_ids, medium_filter, weight, cotangent, feats, feats, feats, filters, filters, filters)
 
 
-def vmem(count):
-    return [pl.BlockSpec(memory_space=pltpu.VMEM)] * count
-
-
-def run_gather(short_filter, counts, plan, replicas, zeros, scale):
+def toeplitz(row, square):
+    return pltpu.roll(jnp.broadcast_to(row, square), 0, 1, stride=1, stride_axis=0)
+
+
+def whole_kernel(
+    replicas, zeros, scale, short, gsize,
+    counts, plan, doc, taps, filt, feats_hbm, cot_hbm,
+    mixed, grads, short_out, medium_out,
+    feats, cot, loaded, rows, stage, slots, tally, tallies, filters,
+    down, up_cat, causal, causal_t, causal_r, flip, tap_rows, tap_back, living, med,
+    forward, backward, grad_short,
+    mpack, mslots, mpart, mparts, share, shares, spack, sslots, spart, sparts,
+    send, recv, tsend, trecv, m1s, m1r, m2s, m2r, m3s, m3r, s1s, s1r, s2s, s2r,
+):
+    barrier = greet(replicas, zeros)
+    mine, place = lax.axis_index("zero"), lax.axis_index("dp")
+    length = cot.shape[0]
+    width = cot.shape[1]
+    cw = filt.shape[1]
+    half = cw // 2
+    per = LANES // gsize
+    square = (length, length)
+    load_feats = pltpu.make_async_copy(feats_hbm, feats, loaded.at[0])
+    load_cot = pltpu.make_async_copy(cot_hbm, cot, loaded.at[1])
+    load_feats.start()
+    load_cot.start()
+
+    lane = lax.broadcasted_iota(jnp.int32, (1, cw), 1)
+    rows[0:short, :] = filt[...].astype(F32)
+    rows[short:8, :] = jnp.where(lane == plan[0], counts[0].astype(F32), 0.0)
+    staged = jnp.concatenate([rows[:, :half], rows[:, half:]], 0).astype(BF16)
+    stage[...] = staged
+    slots[mine] = staged
+    pl.semaphore_wait(barrier, zeros + replicas - 2)
+    gathering = spread("zero", zeros, lambda peer: stage, slots, send, recv)
+
+    r = lax.broadcasted_iota(jnp.int32, square, 0)
+    c = lax.broadcasted_iota(jnp.int32, square, 1)
+    across = jnp.broadcast_to(doc[...].astype(F32), square)
+    same = (across == across.T).astype(F32)
+    for j in range(short):
+        down[j] = jnp.where(r - c == j, same, 0.0).astype(BF16)
+        up_cat[:, j * length : (j + 1) * length] = jnp.where(c - r == j, same, 0.0).astype(BF16)
+    low = jnp.where(r >= c, same, 0.0)
+    causal[...] = low
+    causal_t[...] = jnp.where(c >= r, same, 0.0)
+    turn = (r + c == length - 1).astype(BF16)
+    flip[...] = turn
+    causal_r[...] = dot(low.astype(BF16), turn)
+    rounded = taps[...].astype(BF16).astype(F32).T
+    tap_rows[...] = rounded
+    back = (lax.rem(r + c, length) == 0).astype(BF16)
+    tap_back[...] = dot(rounded.astype(BF16), back)
+    living[...] = (r < counts[0]).astype(F32)
+
+    def build(block, carry):
+        back8 = tap_back[pl.ds(pl.multiple_of(block * per, per), per), :]
+        rows8 = tap_rows[pl.ds(pl.multiple_of(block * per, per), per), :]
+        for i in range(per):
+            at = slice(i * length, (i + 1) * length)
+            one = toeplitz(back8[i : i + 1], square)
+            forward[block, :, at] = (one * causal[...]).astype(BF16)
+            two = toeplitz(rows8[i : i + 1], square)
+            backward[block, :, at] = (two * causal_t[...]).astype(BF16)
+        return carry
+
+    lax.fori_loop(0, width // LANES, build, 0)
+
+    for copy in gathering:
+        copy.wait()
+    total = slots[0].astype(F32)[short : short + 1, :LANES]
+    for z in range(1, zeros):
+        total = total + slots[z].astype(F32)[short : short + 1, :LANES]
+    tally[...] = jnp.broadcast_to(total, (8, LANES))
+    tallies[place] = jnp.broadcast_to(total, (8, LANES))
+    counting = spread("dp", replicas, lambda peer: tally, tallies, tsend, trecv)
+    for z in range(zeros):
+        block = slots[z].astype(F32)
+        filters[:, z * cw : z * cw + half] = block[0:8]
+        filters[:, z * cw + half : (z + 1) * cw] = block[8:16]
+    load_feats.wait()
+    load_cot.wait()
+
+    group = lax.broadcasted_iota(jnp.int32, (1, LANES), 1) // gsize
+    picks = [(group == i).astype(BF16) for i in range(per)]
+
+    def blocks(step, carry):
+        def convolve(n):
+            where = pl.ds(pl.multiple_of(n * width + step * WIDE, LANES), WIDE)
+            x = feats[:, where]
+            taps7 = filters[:, where]
+            total = taps7[0:1] * x.astype(F32)
+            for j in range(1, short):
+                total = total + taps7[j : j + 1] * dot(down[j], x)
+            return total
+
+        query, key, value = convolve(0), convolve(1), convolve(2)
+        for h in range(WIDE // LANES):
+            cols = slice(h * LANES, (h + 1) * LANES)
+            q, k, v = query[:, cols], key[:, cols], value[:, cols]
+            begin = pl.multiple_of(step * WIDE + h * LANES, LANES)
+            here = pl.ds(begin, LANES)
+            product = (k * v).astype(BF16)
+            block = step * (WIDE // LANES) + h
+            long_conv = dot(forward[block], jnp.concatenate([product * m for m in picks], 0))
+            alive = living[...]
+            mixed[:, here] = (alive * q * long_conv).astype(BF16)
+            grad_out = cot[:, here].astype(F32) * alive
+            grad_long = (grad_out * q).astype(BF16)
+            chosen = jnp.concatenate([grad_long * m for m in picks], 0)
+            grad_product = dot(backward[block], chosen)
+            turned = dot(flip[...], product).astype(BF16)
+            crossed = lax.dot_general(
+                chosen, turned, (((1,), (1,)), ((), ())), preferred_element_type=F32
+            )
+            for i in range(per):
+                part = crossed[i * length : (i + 1) * length] * causal_r[...]
+                part = pltpu.roll(part, 1, 1, stride=1, stride_axis=0)
+                med[pl.ds(block * per + i, 1), :] = jnp.sum(part, 0, keepdims=True)
+            grad_short[:, here] = (grad_out * long_conv).astype(BF16)
+            there = pl.ds(pl.multiple_of(begin + width, LANES), LANES)
+            grad_short[:, there] = (grad_product * v).astype(BF16)
+            there = pl.ds(pl.multiple_of(begin + 2 * width, LANES), LANES)
+            grad_short[:, there] = (grad_product * k).astype(BF16)
+        return carry
+
+    lax.fori_loop(0, width // WIDE, blocks, 0)
+
+    for copy in counting:
+        copy.wait()
+    total = tallies[0]
+    for p in range(1, replicas):
+        total = total + tallies[p]
+    lane8 = lax.broadcasted_iota(jnp.int32, (8, LANES), 1)
+    own = jnp.sum(jnp.where(lane8 == plan[0], total, 0.0), 1, keepdims=True)
+    weight = (scale / own)[0:1]
+
+    depth = taps.shape[0] // zeros
+    medium = med[...].T * weight
+    for z in range(zeros):
+        mpack[z] = medium[z * depth : (z + 1) * depth].astype(BF16)
+    mslots[mine] = mpack[mine]
+    medium_one = spread("zero", zeros, lambda peer: mpack.at[peer], mslots, m1s, m1r)
+
+    def short_chunk(owner):
+        sums = []
+        for s in range(cw // WIDE):
+            where = pl.ds(pl.multiple_of(owner * cw + s * WIDE, LANES), WIDE)
+            x = feats[:, where]
+            grad = grad_short[:, where].astype(F32)
+            lines = [jnp.sum(grad * x.astype(F32), 0, keepdims=True)]
+            for j in range(1, short):
+                lines.append(jnp.sum(grad * dot(down[j], x), 0, keepdims=True))
+            lines.append(jnp.zeros((8 - short, WIDE), F32))
+            sums.append(jnp.concatenate(lines, 0))
+        both = jnp.concatenate(sums, 1) * weight
+        return jnp.concatenate([both[:, :half], both[:, half:]], 0).astype(BF16)
+
+    def short_copy(step):
+        peer = lax.rem(mine + step, zeros)
+        return pltpu.make_async_remote_copy(
+            src_ref=spack.at[peer],
+            dst_ref=sslots.at[mine],
+            send_sem=s1s.at[step],
+            recv_sem=s1r.at[step],
+            device_id={"zero": peer},
+            device_id_type=MESH,
+        )
+
+    def send_short(step, carry):
+        peer = lax.rem(mine + step, zeros)
+        spack[peer] = short_chunk(peer)
+        short_copy(step).start()
+        return carry
+
+    lax.fori_loop(1, zeros, send_short, 0)
+    sslots[mine] = short_chunk(mine)
+
+    for copy in medium_one:
+        copy.wait()
+    total = mslots[0].astype(F32)
+    for z in range(1, zeros):
+        total = total + mslots[z].astype(F32)
+    mpart[...] = total
+    mparts[place] = total
+    medium_two = spread("dp", replicas, lambda peer: mpart, mparts, m2s, m2r)
+
+    def feats_chunk(index, carry):
+        where = pl.ds(pl.multiple_of(index * WIDE, LANES), WIDE)
+        grad = grad_short[:, where]
+        taps7 = filters[:, where].astype(BF16)
+        scaled = jnp.concatenate([grad * taps7[j : j + 1] for j in range(short)], 0)
+        grads[:, where] = (dot(up_cat[...], scaled) * weight).astype(BF16)
+        return carry
+
+    pieces = 3 * width // WIDE
+    lax.fori_loop(0, pieces // 2, feats_chunk, 0)
+
+    for step in range(1, zeros):
+        short_copy(step).wait()
+    total = sslots[0].astype(F32)
+    for z in range(1, zeros):
+        total = total + sslots[z].astype(F32)
+    spart[...] = total
+    sparts[place] = total
+    short_two = spread("dp", replicas, lambda peer: spart, sparts, s2s, s2r)
+    for copy in medium_two:
+        copy.wait()
+    total = mparts[0]
+    for p in range(1, replicas):
+        total = total + mparts[p]
+    share[...] = total
+    shares[mine] = total
+    medium_three = spread("zero", zeros, lambda peer: share, shares, m3s, m3r)
+
+    lax.fori_loop(pieces // 2, pieces, feats_chunk, 0)
+
+    for copy in short_two:
+        copy.wait()
+    total = sparts[0]
+    for p in range(1, replicas):
+        total = total + sparts[p]
+    short_out[:, :half] = total[0:short]
+    short_out[:, half:] = total[8 : 8 + short]
+    for copy in medium_three:
+        copy.wait()
+    for z in range(zeros):
+        medium_out[z * depth : (z + 1) * depth, :] = shares[z]
+
+
+def run_whole(feats, short_filter, medium_filter, doc_ids, counts, plan, cotangent, replicas, zeros, scale):
+    length, width = cotangent.shape
     short, cw = short_filter.shape
     half = cw // 2
+    taps_count, groups = medium_filter.shape
+    depth = taps_count // zeros
+    square = (length, length)
+    gsize = width // groups
+    in_vmem = pl.BlockSpec(memory_space=pltpu.VMEM)
+    in_smem = pl.BlockSpec(memory_space=pltpu.SMEM)
+    anywhere = pl.BlockSpec(memory_space=pl.ANY)
+    stacked = (width // LANES, length, LANES // gsize * length)
+    along_zero, along_dp = pltpu.SemaphoreType.DMA((zeros,)), pltpu.SemaphoreType.DMA((replicas,))
     return pl.pallas_call(
-        functools.partial(gather_kernel, replicas, zeros, scale, short),
-        in_specs=vmem(1) + [pl.BlockSpec(memory_space=pltpu.SMEM)] * 2,
-        out_specs=vmem(2),
+        functools.partial(whole_kernel, replicas, zeros, scale, short, gsize),
+        in_specs=[in_smem, in_smem, in_vmem, in_vmem, in_vmem, anywhere, anywhere],
+        out_specs=[in_vmem] * 4,
         out_shape=[
-            jax.ShapeDtypeStruct((8, cw * zeros), F32),
-            jax.ShapeDtypeStruct((8, LANES), F32),
+            jax.ShapeDtypeStruct((length, width), BF16),
+            jax.ShapeDtypeStruct(feats.shape, BF16),
+            jax.ShapeDtypeStruct((short, cw), F32),
+            jax.ShapeDtypeStruct((taps_count, groups), F32),
         ],
         scratch_shapes=[
+            pltpu.VMEM(feats.shape, BF16),
+            pltpu.VMEM((length, width), BF16),
+            pltpu.SemaphoreType.DMA((2,)),
             pltpu.VMEM((8, cw), F32),
             pltpu.VMEM((16, half), BF16),
             pltpu.VMEM((zeros, 16, half), BF16),
             pltpu.VMEM((8, LANES), F32),
             pltpu.VMEM((replicas, 8, LANES), F32),
-            pltpu.SemaphoreType.DMA((zeros,)),
-            pltpu.SemaphoreType.DMA((zeros,)),
-            pltpu.SemaphoreType.DMA((replicas,)),
-            pltpu.SemaphoreType.DMA((replicas,)),
-        ],
-        compiler_params=pltpu.CompilerParams(collective_id=0, has_side_effects=True),
-        name="gather_filters",
-    )(short_filter, counts, plan)
-
-
-def run_reduce(shorts, medium, replicas, zeros, short):
-    cw = shorts.shape[1] // zeros
-    half = cw // 2
-    taps_count, groups = medium.shape
-    depth = taps_count // zeros
-    return pl.pallas_call(
-        functools.partial(reduce_kernel, replicas, zeros, short),
-        in_specs=vmem(2),
-        out_specs=vmem(2),
-        out_shape=[
-            jax.ShapeDtypeStruct((short, cw), F32),
-            jax.ShapeDtypeStruct((taps_count, groups), F32),
-        ],
-        scratch_shapes=[
-            pltpu.VMEM((zeros, 16, half + groups), BF16),
-            pltpu.VMEM((zeros, 16, half + groups), BF16),
-            pltpu.VMEM((16, half + groups), F32),
-            pltpu.VMEM((replicas, 16, half + groups), F32),
+            pltpu.VMEM((8, 3 * width), F32),
+            pltpu.VMEM((short, length, length), BF16),
+            pltpu.VMEM((length, short * length), BF16),
+            pltpu.VMEM(square, F32),
+            pltpu.VMEM(square, F32),
+            pltpu.VMEM(square, F32),
+            pltpu.VMEM(square, BF16),
+            pltpu.VMEM((groups, taps_count), F32),
+            pltpu.VMEM((groups, taps_count), F32),
+            pltpu.VMEM((length, LANES), F32),
+            pltpu.VMEM((groups, taps_count), F32),
+            pltpu.VMEM(stacked, BF16),
+            pltpu.VMEM(stacked, BF16),
+            pltpu.VMEM(feats.shape, BF16),
+            pltpu.VMEM((zeros, depth, groups), BF16),
+            pltpu.VMEM((zeros, depth, groups), BF16),
+            pltpu.VMEM((depth, groups), F32),
+            pltpu.VMEM((replicas, depth, groups), F32),
             pltpu.VMEM((depth, groups), F32),
             pltpu.VMEM((zeros, depth, groups), F32),
-            pltpu.SemaphoreType.DMA((zeros,)),
-            pltpu.SemaphoreType.DMA((zeros,)),
-            pltpu.SemaphoreType.DMA((replicas,)),
-            pltpu.SemaphoreType.DMA((replicas,)),
-            pltpu.SemaphoreType.DMA((zeros,)),
-            pltpu.SemaphoreType.DMA((zeros,)),
+            pltpu.VMEM((zeros, 16, half), BF16),
+            pltpu.VMEM((zeros, 16, half), BF16),
+            pltpu.VMEM((16, half), F32),
+            pltpu.VMEM((replicas, 16, half), F32),
+            along_zero, along_zero, along_dp, along_dp,
+            along_zero, along_zero, along_dp, along_dp, along_zero, along_zero,
+            along_zero, along_zero, along_dp, along_dp,
         ],
-        compiler_params=pltpu.CompilerParams(collective_id=1, has_side_effects=True),
-        name="reduce_filters",
-    )(shorts, medium)
+        compiler_params=pltpu.CompilerParams(
+            collective_id=0, has_side_effects=True, vmem_limit_bytes=56 * 1024 * 1024
+        ),
+        name="whole_block",
+    )(counts, plan, doc_ids, medium_filter, short_filter, feats, cotangent)
+
+
+def hand_kernel(count, *refs):
+    sources, targets, done = refs[:count], refs[count : 2 * count], refs[2 * count]
+    copies = []
+    for n in range(count):
+        rows = sources[n].shape[0]
+        cuts = 4 if rows % 64 == 0 else 1
+        for cut in range(cuts):
+            part = pl.ds(cut * rows // cuts, rows // cuts)
+            source, target = sources[n].at[part], targets[n].at[part]
+            copies.append(pltpu.make_async_copy(source, target, done.at[len(copies)]))
+    for copy in copies:
+        copy.start()
+    for copy in copies:
+        copy.wait()
+
+
+def hand_over(arrays):
+    anywhere = pl.BlockSpec(memory_space=pl.ANY)
+    return pl.pallas_call(
+        functools.partial(hand_kernel, len(arrays)),
+        in_specs=[anywhere] * len(arrays),
+        out_specs=[anywhere] * len(arrays),
+        out_shape=[jax.ShapeDtypeStruct(a.shape, a.dtype) for a in arrays],
+        scratch_shapes=[pltpu.SemaphoreType.DMA((4 * len(arrays),))],
+        compiler_params=pltpu.CompilerParams(vmem_limit_bytes=56 * 1024 * 1024),
+        name="hand_over",
+    )(*arrays)
 
 
 def shards(feats, short_filter, medium_filter, doc_ids, counts, plan, cotangent):
@@ -343,23 +528,21 @@
     scale = float(length * replicas * zeros / replicas)
     packed = cw % WIDE == 0 and medium_filter.shape[0] == 16 * zeros
     if packed:
-        filters, weight = run_gather(short_filter, counts, plan, replicas, zeros, scale)
-    else:
-        member = (plan[0] == jnp.arange(replicas)).astype(F32)
-        totals = lax.psum(member * counts[0].astype(F32), ("dp", "zero"))
-        weight = jnp.broadcast_to(scale / jnp.sum(member * totals), (8, LANES))
-        filters = lax.all_gather(short_filter, "zero", axis=1, tiled=True).astype(F32)
-        filters = jnp.pad(filters, ((0, 8 - short), (0, 0)))
+        return hand_over(run_whole(
+            feats, short_filter, medium_filter, doc_ids, counts, plan, cotangent, replicas, zeros, scale
+        ))
+    member = (plan[0] == jnp.arange(replicas)).astype(F32)
+    totals = lax.psum(member * counts[0].astype(F32), ("dp", "zero"))
+    weight = jnp.broadcast_to(scale / jnp.sum(member * totals), (8, LANES))
+    filters = lax.all_gather(short_filter, "zero", axis=1, tiled=True).astype(F32)
+    filters = jnp.pad(filters, ((0, 8 - short), (0, 0)))
     mixed, grads, shorts, medium = run_block(
         feats, filters, medium_filter, doc_ids, counts, weight, cotangent, short
     )
-    if packed:
-        short_grad, medium_grad = run_reduce(shorts, medium, replicas, zeros, short)
-    else:
-        own = lax.psum(shorts[:short], "dp")
-        own = own.reshape(short, zeros, cw).transpose(1, 0, 2)
-        short_grad = lax.psum_scatter(own, "zero", scatter_dimension=0, tiled=True)[0]
-        medium_grad = lax.psum(medium, ("dp", "zero"))
+    own = lax.psum(shorts[:short], "dp")
+    own = own.reshape(short, zeros, cw).transpose(1, 0, 2)
+    short_grad = lax.psum_scatter(own, "zero", scatter_dimension=0, tiled=True)[0]
+    medium_grad = lax.psum(medium, ("dp", "zero"))
     return mixed, grads, short_grad, medium_grad
 
 

time: 58.3 us -> 107 us (1.84)
  Pallas kernels: 46.2 us -> 105 us
  local copies, waits for them, and re-layouts: 9.67 us -> 0 us
    pallas_call x3 -> x2, Pallas kernels: 46.2 us -> 105 us  [the longest x1 67.5 us: hand_over(): pl.pallas_call(functools.partial(hand_kernel, len(arrays)), in_specs=[any...]
    unnamed x18 -> x0, local copies, waits for them, and re-layouts: 9.67 us -> none
where the time goes in v2:
time: 107 us
  Pallas kernels  105 us (98%)
  between operations  1.93 us (2%)
    pallas_call x1, Pallas kernels, hand_over(): pl.pallas_call(functools.partial(hand_kernel, len(arrays)), in_specs=[any...  67.5 us
    pallas_call x1, Pallas kernels, run_whole(): pl.pallas_call(functools.partial(whole_kernel, replicas, zeros, scale, sh...  37.4 us

profile of v2, /device:TPU:0, one launch (start us, length us, event | category | flops | bytes accessed | tf_op | source)
XLA Modules:
  0.0 106.8 jit_solution(15606027428203445649)
XLA Ops:
  1.9 37.4 %whole_block.1 = (bf16[128,2048]{1,0:T(8,128)(2,1)}, bf16[128,6144]{1,0:T(8,128)(2,1)}, f32[7,768]{1,0:T(8,128)}, f32[128,128]{1,0:T(8,128)}) custom-call(s32[1]{0:T(128)S(6)} %copy.11.counts, s32[1]{0:T(128)S(6)} %copy.12.plan, s32[1,128]{1,0:T(1,128)} %doc.1, f32[128,128]{1,0:T(8,128)} %taps.1, bf16[7,768]{1,0:T(8,128)(2,1)} %filt.1, ...), custom_call_target="tpu_custom_call" | custom-call | tf_op jit(solution)/shard_map/whole_block/pallas_call | solution.py:440
  39.3 67.5 %hand_over.1 = (bf16[128,2048]{1,0:T(8,128)(2,1)}, bf16[128,6144]{1,0:T(8,128)(2,1)}, f32[7,768]{1,0:T(8,128)}, f32[128,128]{1,0:T(8,128)}) custom-call(bf16[128,2048]{1,0:T(8,128)(2,1)} %get-tuple-element.8.refs_0_, bf16[128,6144]{1,0:T(8,128)(2,1)} %get-tuple-element.9.refs_1_, f32[7,768]{1,0:T(8,128)} %get-tuple-element.10.refs_2_, ...), custom_call_target="tpu_custom_call" | custom-call | tf_op jit(solution)/shard_map/hand_over/pallas_call | solution.py:512

commit v3 on v2

--- a/solution.py
+++ b/solution.py
@@ -194,16 +194,16 @@
     )(counts, doc_ids, medium_filter, weight, cotangent, feats, feats, feats, filters, filters, filters)
 
 
-def toeplitz(row, square):
-    return pltpu.roll(jnp.broadcast_to(row, square), 0, 1, stride=1, stride_axis=0)
+def toeplitz(tile, length):
+    return jnp.concatenate([pltpu.roll(tile, at, 1) if at else tile for at in range(0, length, 8)], 0)
 
 
 def whole_kernel(
     replicas, zeros, scale, short, gsize,
     counts, plan, doc, taps, filt, feats_hbm, cot_hbm,
-    mixed, grads, short_out, medium_out,
-    feats, cot, loaded, rows, stage, slots, tally, tallies, filters,
-    down, up_cat, causal, causal_t, causal_r, flip, tap_rows, tap_back, living, med,
+    mixed_hbm, grads_hbm, short_out, medium_out,
+    mixed, grads, feats, cot, loaded, rows, stage, slots, tally, tallies, filters,
+    down, up_cat, causal, causal_t, causal_r, flip, base_rows, base_back, living, med,
     forward, backward, grad_short,
     mpack, mslots, mpart, mparts, share, shares, spack, sslots, spart, sparts,
     send, recv, tsend, trecv, m1s, m1r, m2s, m2r, m3s, m3r, s1s, s1r, s2s, s2r,
@@ -244,19 +244,23 @@
     flip[...] = turn
     causal_r[...] = dot(low.astype(BF16), turn)
     rounded = taps[...].astype(BF16).astype(F32).T
-    tap_rows[...] = rounded
+    tap_rows = rounded
     back = (lax.rem(r + c, length) == 0).astype(BF16)
-    tap_back[...] = dot(rounded.astype(BF16), back)
+    tap_back = dot(rounded.astype(BF16), back)
     living[...] = (r < counts[0]).astype(F32)
 
+    for a in range(8):
+        lines = pl.ds(a, taps.shape[1], stride=8)
+        base_back[lines, :] = pltpu.roll(tap_back, a, 1)
+        base_rows[lines, :] = pltpu.roll(tap_rows, a, 1)
+
     def build(block, carry):
-        back8 = tap_back[pl.ds(pl.multiple_of(block * per, per), per), :]
-        rows8 = tap_rows[pl.ds(pl.multiple_of(block * per, per), per), :]
         for i in range(per):
             at = slice(i * length, (i + 1) * length)
-            one = toeplitz(back8[i : i + 1], square)
+            tile = pl.ds(pl.multiple_of((block * per + i) * 8, 8), 8)
+            one = toeplitz(base_back[tile, :], length)
             forward[block, :, at] = (one * causal[...]).astype(BF16)
-            two = toeplitz(rows8[i : i + 1], square)
+            two = toeplitz(base_rows[tile, :], length)
             backward[block, :, at] = (two * causal_t[...]).astype(BF16)
         return carry
 
@@ -311,8 +315,10 @@
             )
             for i in range(per):
                 part = crossed[i * length : (i + 1) * length] * causal_r[...]
-                part = pltpu.roll(part, 1, 1, stride=1, stride_axis=0)
-                med[pl.ds(block * per + i, 1), :] = jnp.sum(part, 0, keepdims=True)
+                summed = part[0:8]
+                for at in range(8, length, 8):
+                    summed = summed + pltpu.roll(part[at : at + 8], at, 1)
+                med[pl.ds(pl.multiple_of((block * per + i) * 8, 8), 8), :] = summed
             grad_short[:, here] = (grad_out * long_conv).astype(BF16)
             there = pl.ds(pl.multiple_of(begin + width, LANES), LANES)
             grad_short[:, there] = (grad_product * v).astype(BF16)
@@ -321,6 +327,8 @@
         return carry
 
     lax.fori_loop(0, width // WIDE, blocks, 0)
+    save_mixed = pltpu.make_async_copy(mixed, mixed_hbm, loaded.at[2])
+    save_mixed.start()
 
     for copy in counting:
         copy.wait()
@@ -332,7 +340,11 @@
     weight = (scale / own)[0:1]
 
     depth = taps.shape[0] // zeros
-    medium = med[...].T * weight
+    total = None
+    for a in range(8):
+        part = pltpu.roll(med[pl.ds(a, taps.shape[1], stride=8), :], a + 1, 1)
+        total = part if total is None else total + part
+    medium = total.T * weight
     for z in range(zeros):
         mpack[z] = medium[z * depth : (z + 1) * depth].astype(BF16)
     mslots[mine] = mpack[mine]
@@ -390,7 +402,11 @@
         return carry
 
     pieces = 3 * width // WIDE
+    middle = pieces // 2 * WIDE
     lax.fori_loop(0, pieces // 2, feats_chunk, 0)
+    cols = slice(0, middle)
+    save_one = pltpu.make_async_copy(grads.at[:, cols], grads_hbm.at[:, cols], loaded.at[3])
+    save_one.start()
 
     for step in range(1, zeros):
         short_copy(step).wait()
@@ -410,6 +426,9 @@
     medium_three = spread("zero", zeros, lambda peer: share, shares, m3s, m3r)
 
     lax.fori_loop(pieces // 2, pieces, feats_chunk, 0)
+    cols = slice(middle, 3 * width)
+    save_two = pltpu.make_async_copy(grads.at[:, cols], grads_hbm.at[:, cols], loaded.at[4])
+    save_two.start()
 
     for copy in short_two:
         copy.wait()
@@ -422,6 +441,9 @@
         copy.wait()
     for z in range(zeros):
         medium_out[z * depth : (z + 1) * depth, :] = shares[z]
+    save_mixed.wait()
+    save_one.wait()
+    save_two.wait()
 
 
 def run_whole(feats, short_filter, medium_filter, doc_ids, counts, plan, cotangent, replicas, zeros, scale):
@@ -440,7 +462,7 @@
     return pl.pallas_call(
         functools.partial(whole_kernel, replicas, zeros, scale, short, gsize),
         in_specs=[in_smem, in_smem, in_vmem, in_vmem, in_vmem, anywhere, anywhere],
-        out_specs=[in_vmem] * 4,
+        out_specs=[anywhere, anywhere, in_vmem, in_vmem],
         out_shape=[
             jax.ShapeDtypeStruct((length, width), BF16),
             jax.ShapeDtypeStruct(feats.shape, BF16),
@@ -448,9 +470,11 @@
             jax.ShapeDtypeStruct((taps_count, groups), F32),
         ],
         scratch_shapes=[
+            pltpu.VMEM((length, width), BF16),
+            pltpu.VMEM(feats.shape, BF16),
             pltpu.VMEM(feats.shape, BF16),
             pltpu.VMEM((length, width), BF16),
-            pltpu.SemaphoreType.DMA((2,)),
+            pltpu.SemaphoreType.DMA((5,)),
             pltpu.VMEM((8, cw), F32),
             pltpu.VMEM((16, half), BF16),
             pltpu.VMEM((zeros, 16, half), BF16),
@@ -463,10 +487,10 @@
             pltpu.VMEM(square, F32),
             pltpu.VMEM(square, F32),
             pltpu.VMEM(square, BF16),
-            pltpu.VMEM((groups, taps_count), F32),
-            pltpu.VMEM((groups, taps_count), F32),
+            pltpu.VMEM((8 * groups, taps_count), F32),
+            pltpu.VMEM((8 * groups, taps_count), F32),
             pltpu.VMEM((length, LANES), F32),
-            pltpu.VMEM((groups, taps_count), F32),
+            pltpu.VMEM((8 * groups, taps_count), F32),
             pltpu.VMEM(stacked, BF16),
             pltpu.VMEM(stacked, BF16),
             pltpu.VMEM(feats.shape, BF16),
@@ -492,29 +516,23 @@
 
 
 def hand_kernel(count, *refs):
-    sources, targets, done = refs[:count], refs[count : 2 * count], refs[2 * count]
-    copies = []
-    for n in range(count):
-        rows = sources[n].shape[0]
-        cuts = 4 if rows % 64 == 0 else 1
-        for cut in range(cuts):
-            part = pl.ds(cut * rows // cuts, rows // cuts)
-            source, target = sources[n].at[part], targets[n].at[part]
-            copies.append(pltpu.make_async_copy(source, target, done.at[len(copies)]))
-    for copy in copies:
-        copy.start()
-    for copy in copies:
-        copy.wait()
+    for source, target in zip(refs[:count], refs[count:]):
+        target[...] = source[...]
 
 
 def hand_over(arrays):
-    anywhere = pl.BlockSpec(memory_space=pl.ANY)
+    length, parts = arrays[0].shape[0], 4
+    specs = []
+    for a in arrays[:2]:
+        specs.append(pl.BlockSpec((length // parts, a.shape[1]), lambda i: (i, 0)))
+    for a in arrays[2:]:
+        specs.append(pl.BlockSpec(a.shape, lambda i: (0, 0)))
     return pl.pallas_call(
         functools.partial(hand_kernel, len(arrays)),
-        in_specs=[anywhere] * len(arrays),
-        out_specs=[anywhere] * len(arrays),
+        grid=(parts,),
+        in_specs=specs,
+        out_specs=specs,
         out_shape=[jax.ShapeDtypeStruct(a.shape, a.dtype) for a in arrays],
-        scratch_shapes=[pltpu.SemaphoreType.DMA((4 * len(arrays),))],
         compiler_params=pltpu.CompilerParams(vmem_limit_bytes=56 * 1024 * 1024),
         name="hand_over",
     )(*arrays)

time: 107 us -> 43 us (0.40)
  Pallas kernels: 105 us -> 40.8 us
    pallas_call x1, Pallas kernels: 67.5 us -> 3.85 us  [hand_over(): pl.pallas_call(functools.partial(hand_kernel, len(arrays)), grid=(parts,)...]
where the time goes in v3:
time: 43 us; the launch traced here: 42.8 us
  Pallas kernels  40.8 us (95%)
  between operations  1.93 us (4%)
    pallas_call x1, Pallas kernels, run_whole(): pl.pallas_call(functools.partial(whole_kernel, replicas, zeros, scale, sh...  37 us
    pallas_call x1, Pallas kernels, hand_over(): pl.pallas_call(functools.partial(hand_kernel, len(arrays)), grid=(parts,)...  3.85 us

profile of v3, /device:TPU:0, one launch (start us, length us, event | category | flops | bytes accessed | tf_op | source)
XLA Modules:
  0.0 42.8 jit_solution(14783402129435589407)
XLA Ops:
  1.9 37.0 %whole_block.1 = (bf16[128,2048]{1,0:T(8,128)(2,1)}, bf16[128,6144]{1,0:T(8,128)(2,1)}, f32[7,768]{1,0:T(8,128)}, f32[128,128]{1,0:T(8,128)}) custom-call(s32[1]{0:T(128)S(6)} %copy.11.counts, s32[1]{0:T(128)S(6)} %copy.12.plan, s32[1,128]{1,0:T(1,128)} %doc.1, f32[128,128]{1,0:T(8,128)} %taps.1, bf16[7,768]{1,0:T(8,128)(2,1)} %filt.1, ...), custom_call_target="tpu_custom_call" | custom-call | tf_op jit(solution)/shard_map/whole_block/pallas_call | solution.py:462
  38.9 3.8 %hand_over.1 = (bf16[128,2048]{1,0:T(8,128)(2,1)}, bf16[128,6144]{1,0:T(8,128)(2,1)}, f32[7,768]{1,0:T(8,128)}, f32[128,128]{1,0:T(8,128)}) custom-call(bf16[128,2048]{1,0:T(8,128)(2,1)} %get-tuple-element.8.refs_0_, bf16[128,6144]{1,0:T(8,128)(2,1)} %get-tuple-element.9.refs_1_, f32[7,768]{1,0:T(8,128)} %get-tuple-element.10.refs_2_, ...), custom_call_target="tpu_custom_call" | custom-call | tf_op jit(solution)/shard_map/hand_over/pallas_call | solution.py:530

commit v4 on v3

--- a/solution.py
+++ b/solution.py
@@ -204,7 +204,7 @@
     mixed_hbm, grads_hbm, short_out, medium_out,
     mixed, grads, feats, cot, loaded, rows, stage, slots, tally, tallies, filters,
     down, up_cat, causal, causal_t, causal_r, flip, base_rows, base_back, living, med,
-    forward, backward, grad_short,
+    forward, backward, grad_short, moved, crossing,
     mpack, mslots, mpart, mparts, share, shares, spack, sslots, spart, sparts,
     send, recv, tsend, trecv, m1s, m1r, m2s, m2r, m3s, m3r, s1s, s1r, s2s, s2r,
 ):
@@ -235,7 +235,8 @@
     across = jnp.broadcast_to(doc[...].astype(F32), square)
     same = (across == across.T).astype(F32)
     for j in range(short):
-        down[j] = jnp.where(r - c == j, same, 0.0).astype(BF16)
+        if j:
+            down[(j - 1) * length : j * length, :] = jnp.where(r - c == j, same, 0.0).astype(BF16)
         up_cat[:, j * length : (j + 1) * length] = jnp.where(c - r == j, same, 0.0).astype(BF16)
     low = jnp.where(r >= c, same, 0.0)
     causal[...] = low
@@ -266,6 +267,16 @@
 
     lax.fori_loop(0, width // LANES, build, 0)
 
+    load_feats.wait()
+
+    def shift(index, carry):
+        where = pl.ds(pl.multiple_of(index * WIDE, LANES), WIDE)
+        moved[:, where] = dot(down[...], feats[:, where]).astype(BF16)
+        return carry
+
+    lax.fori_loop(0, 3 * width // WIDE, shift, 0)
+    crossing[...] = jnp.zeros_like(crossing)
+
     for copy in gathering:
         copy.wait()
     total = slots[0].astype(F32)[short : short + 1, :LANES]
@@ -278,7 +289,6 @@
         block = slots[z].astype(F32)
         filters[:, z * cw : z * cw + half] = block[0:8]
         filters[:, z * cw + half : (z + 1) * cw] = block[8:16]
-    load_feats.wait()
     load_cot.wait()
 
     group = lax.broadcasted_iota(jnp.int32, (1, LANES), 1) // gsize
@@ -291,7 +301,8 @@
             taps7 = filters[:, where]
             total = taps7[0:1] * x.astype(F32)
             for j in range(1, short):
-                total = total + taps7[j : j + 1] * dot(down[j], x)
+                at = slice((j - 1) * length, j * length)
+                total = total + taps7[j : j + 1] * moved[at, where].astype(F32)
             return total
 
         query, key, value = convolve(0), convolve(1), convolve(2)
@@ -309,12 +320,15 @@
             grad_long = (grad_out * q).astype(BF16)
             chosen = jnp.concatenate([grad_long * m for m in picks], 0)
             grad_product = dot(backward[block], chosen)
-            turned = dot(flip[...], product).astype(BF16)
-            crossed = lax.dot_general(
-                chosen, turned, (((1,), (1,)), ((), ())), preferred_element_type=F32
-            )
+            turned = lax.dot_general(
+                product, flip[...], (((0,), (0,)), ((), ())), preferred_element_type=F32
+            ).astype(BF16)
             for i in range(per):
-                part = crossed[i * length : (i + 1) * length] * causal_r[...]
+                at = slice(i * gsize, (i + 1) * gsize)
+                crossing[h, at, i * length : (i + 1) * length] = turned[at]
+            crossed = dot(grad_long, crossing[h])
+            for i in range(per):
+                part = crossed[:, i * length : (i + 1) * length] * causal_r[...]
                 summed = part[0:8]
                 for at in range(8, length, 8):
                     summed = summed + pltpu.roll(part[at : at + 8], at, 1)
@@ -358,7 +372,8 @@
             grad = grad_short[:, where].astype(F32)
             lines = [jnp.sum(grad * x.astype(F32), 0, keepdims=True)]
             for j in range(1, short):
-                lines.append(jnp.sum(grad * dot(down[j], x), 0, keepdims=True))
+                at = slice((j - 1) * length, j * length)
+                lines.append(jnp.sum(grad * moved[at, where].astype(F32), 0, keepdims=True))
             lines.append(jnp.zeros((8 - short, WIDE), F32))
             sums.append(jnp.concatenate(lines, 0))
         both = jnp.concatenate(sums, 1) * weight
@@ -481,7 +496,7 @@
             pltpu.VMEM((8, LANES), F32),
             pltpu.VMEM((replicas, 8, LANES), F32),
             pltpu.VMEM((8, 3 * width), F32),
-            pltpu.VMEM((short, length, length), BF16),
+            pltpu.VMEM(((short - 1) * length, length), BF16),
             pltpu.VMEM((length, short * length), BF16),
             pltpu.VMEM(square, F32),
             pltpu.VMEM(square, F32),
@@ -494,6 +509,8 @@
             pltpu.VMEM(stacked, BF16),
             pltpu.VMEM(stacked, BF16),
             pltpu.VMEM(feats.shape, BF16),
+            pltpu.VMEM(((short - 1) * length, 3 * width), BF16),
+            pltpu.VMEM((WIDE // LANES, LANES, LANES // gsize * length), BF16),
             pltpu.VMEM((zeros, depth, groups), BF16),
             pltpu.VMEM((zeros, depth, groups), BF16),
             pltpu.VMEM((depth, groups), F32),

time: 43 us -> 47.1 us (1.095)
  Pallas kernels: 40.8 us -> 45 us
    pallas_call x1, Pallas kernels: 37 us -> 41.1 us  [run_whole(): pl.pallas_call(functools.partial(whole_kernel, replicas, zeros, scale, sh...]
where the time goes in v4:
time: 47.1 us; the launch traced here: 46.9 us
  Pallas kernels  45 us (96%)
  between operations  1.93 us (4%)
    pallas_call x1, Pallas kernels, run_whole(): pl.pallas_call(functools.partial(whole_kernel, replicas, zeros, scale, sh...  41.1 us
    pallas_call x1, Pallas kernels, hand_over(): pl.pallas_call(functools.partial(hand_kernel, len(arrays)), grid=(parts,)...  3.85 us

profile of v4, /device:TPU:0, one launch (start us, length us, event | category | flops | bytes accessed | tf_op | source)
XLA Modules:
  0.0 46.9 jit_solution(12583373057485451371)
XLA Ops:
  1.9 41.1 %whole_block.1 = (bf16[128,2048]{1,0:T(8,128)(2,1)}, bf16[128,6144]{1,0:T(8,128)(2,1)}, f32[7,768]{1,0:T(8,128)}, f32[128,128]{1,0:T(8,128)}) custom-call(s32[1]{0:T(128)S(6)} %copy.11.counts, s32[1]{0:T(128)S(6)} %copy.12.plan, s32[1,128]{1,0:T(1,128)} %doc.1, f32[128,128]{1,0:T(8,128)} %taps.1, bf16[7,768]{1,0:T(8,128)(2,1)} %filt.1, ...), custom_call_target="tpu_custom_call" | custom-call | tf_op jit(solution)/shard_map/whole_block/pallas_call | solution.py:477
  43.0 3.8 %hand_over.1 = (bf16[128,2048]{1,0:T(8,128)(2,1)}, bf16[128,6144]{1,0:T(8,128)(2,1)}, f32[7,768]{1,0:T(8,128)}, f32[128,128]{1,0:T(8,128)}) custom-call(bf16[128,2048]{1,0:T(8,128)(2,1)} %get-tuple-element.8.refs_0_, bf16[128,6144]{1,0:T(8,128)(2,1)} %get-tuple-element.9.refs_1_, f32[7,768]{1,0:T(8,128)} %get-tuple-element.10.refs_2_, ...), custom_call_target="tpu_custom_call" | custom-call | tf_op jit(solution)/shard_map/hand_over/pallas_call | solution.py:547

commit v5 on v4

--- a/solution.py
+++ b/solution.py
@@ -203,8 +203,8 @@
     counts, plan, doc, taps, filt, feats_hbm, cot_hbm,
     mixed_hbm, grads_hbm, short_out, medium_out,
     mixed, grads, feats, cot, loaded, rows, stage, slots, tally, tallies, filters,
-    down, up_cat, causal, causal_t, causal_r, flip, base_rows, base_back, living, med,
-    forward, backward, grad_short, moved, crossing,
+    down, down_cat, up_cat, causal, causal_t, causal_r, flip, base_rows, base_back, living, med,
+    forward, backward, grad_short, crossing,
     mpack, mslots, mpart, mparts, share, shares, spack, sslots, spart, sparts,
     send, recv, tsend, trecv, m1s, m1r, m2s, m2r, m3s, m3r, s1s, s1r, s2s, s2r,
 ):
@@ -235,12 +235,14 @@
     across = jnp.broadcast_to(doc[...].astype(F32), square)
     same = (across == across.T).astype(F32)
     for j in range(short):
+        down[j] = jnp.where(r - c == j, same, 0.0).astype(BF16)
         if j:
-            down[(j - 1) * length : j * length, :] = jnp.where(r - c == j, same, 0.0).astype(BF16)
-        up_cat[:, j * length : (j + 1) * length] = jnp.where(c - r == j, same, 0.0).astype(BF16)
+            at = slice((j - 1) * length, j * length)
+            down_cat[:, at] = down[j]
+            up_cat[:, at] = jnp.where(c - r == j, same, 0.0).astype(BF16)
     low = jnp.where(r >= c, same, 0.0)
-    causal[...] = low
-    causal_t[...] = jnp.where(c >= r, same, 0.0)
+    causal[...] = low.astype(BF16)
+    causal_t[...] = jnp.where(c >= r, same, 0.0).astype(BF16)
     turn = (r + c == length - 1).astype(BF16)
     flip[...] = turn
     causal_r[...] = dot(low.astype(BF16), turn)
@@ -260,21 +262,12 @@
             at = slice(i * length, (i + 1) * length)
             tile = pl.ds(pl.multiple_of((block * per + i) * 8, 8), 8)
             one = toeplitz(base_back[tile, :], length)
-            forward[block, :, at] = (one * causal[...]).astype(BF16)
+            forward[block, :, at] = one.astype(BF16) * causal[...]
             two = toeplitz(base_rows[tile, :], length)
-            backward[block, :, at] = (two * causal_t[...]).astype(BF16)
+            backward[block, :, at] = two.astype(BF16) * causal_t[...]
         return carry
 
     lax.fori_loop(0, width // LANES, build, 0)
-
-    load_feats.wait()
-
-    def shift(index, carry):
-        where = pl.ds(pl.multiple_of(index * WIDE, LANES), WIDE)
-        moved[:, where] = dot(down[...], feats[:, where]).astype(BF16)
-        return carry
-
-    lax.fori_loop(0, 3 * width // WIDE, shift, 0)
     crossing[...] = jnp.zeros_like(crossing)
 
     for copy in gathering:
@@ -289,6 +282,7 @@
         block = slots[z].astype(F32)
         filters[:, z * cw : z * cw + half] = block[0:8]
         filters[:, z * cw + half : (z + 1) * cw] = block[8:16]
+    load_feats.wait()
     load_cot.wait()
 
     group = lax.broadcasted_iota(jnp.int32, (1, LANES), 1) // gsize
@@ -299,11 +293,9 @@
             where = pl.ds(pl.multiple_of(n * width + step * WIDE, LANES), WIDE)
             x = feats[:, where]
             taps7 = filters[:, where]
-            total = taps7[0:1] * x.astype(F32)
-            for j in range(1, short):
-                at = slice((j - 1) * length, j * length)
-                total = total + taps7[j : j + 1] * moved[at, where].astype(F32)
-            return total
+            narrow = taps7.astype(BF16)
+            scaled = jnp.concatenate([x * narrow[j : j + 1] for j in range(1, short)], 0)
+            return taps7[0:1] * x.astype(F32) + dot(down_cat[...], scaled)
 
         query, key, value = convolve(0), convolve(1), convolve(2)
         for h in range(WIDE // LANES):
@@ -372,8 +364,7 @@
             grad = grad_short[:, where].astype(F32)
             lines = [jnp.sum(grad * x.astype(F32), 0, keepdims=True)]
             for j in range(1, short):
-                at = slice((j - 1) * length, j * length)
-                lines.append(jnp.sum(grad * moved[at, where].astype(F32), 0, keepdims=True))
+                lines.append(jnp.sum(grad * dot(down[j], x), 0, keepdims=True))
             lines.append(jnp.zeros((8 - short, WIDE), F32))
             sums.append(jnp.concatenate(lines, 0))
         both = jnp.concatenate(sums, 1) * weight
@@ -411,9 +402,11 @@
     def feats_chunk(index, carry):
         where = pl.ds(pl.multiple_of(index * WIDE, LANES), WIDE)
         grad = grad_short[:, where]
-        taps7 = filters[:, where].astype(BF16)
-        scaled = jnp.concatenate([grad * taps7[j : j + 1] for j in range(short)], 0)
-        grads[:, where] = (dot(up_cat[...], scaled) * weight).astype(BF16)
+        taps7 = filters[:, where]
+        narrow = taps7.astype(BF16)
+        scaled = jnp.concatenate([grad * narrow[j : j + 1] for j in range(1, short)], 0)
+        total = taps7[0:1] * grad.astype(F32) + dot(up_cat[...], scaled)
+        grads[:, where] = (total * weight).astype(BF16)
         return carry
 
     pieces = 3 * width // WIDE
@@ -496,10 +489,11 @@
             pltpu.VMEM((8, LANES), F32),
             pltpu.VMEM((replicas, 8, LANES), F32),
             pltpu.VMEM((8, 3 * width), F32),
-            pltpu.VMEM(((short - 1) * length, length), BF16),
-            pltpu.VMEM((length, short * length), BF16),
-            pltpu.VMEM(square, F32),
-            pltpu.VMEM(square, F32),
+            pltpu.VMEM((short, length, length), BF16),
+            pltpu.VMEM((length, (short - 1) * length), BF16),
+            pltpu.VMEM((length, (short - 1) * length), BF16),
+            pltpu.VMEM(square, BF16),
+            pltpu.VMEM(square, BF16),
             pltpu.VMEM(square, F32),
             pltpu.VMEM(square, BF16),
             pltpu.VMEM((8 * groups, taps_count), F32),
@@ -509,7 +503,6 @@
             pltpu.VMEM(stacked, BF16),
             pltpu.VMEM(stacked, BF16),
             pltpu.VMEM(feats.shape, BF16),
-            pltpu.VMEM(((short - 1) * length, 3 * width), BF16),
             pltpu.VMEM((WIDE // LANES, LANES, LANES // gsize * length), BF16),
             pltpu.VMEM((zeros, depth, groups), BF16),
             pltpu.VMEM((zeros, depth, groups), BF16),
@@ -533,23 +526,35 @@
 
 
 def hand_kernel(count, *refs):
-    for source, target in zip(refs[:count], refs[count:]):
-        target[...] = source[...]
+    sources, targets = refs[:count], refs[count : 2 * count]
+    held, came, left = refs[2 * count : 3 * count], refs[3 * count], refs[3 * count + 1]
+    arriving, leaving = [], []
+    for n in range(count):
+        rows = sources[n].shape[0]
+        cuts = 4 if rows % 64 == 0 and n < 2 else 1
+        for cut in range(cuts):
+            part = pl.ds(cut * rows // cuts, rows // cuts)
+            slot, at = held[n].at[part], len(arriving)
+            arriving.append(pltpu.make_async_copy(sources[n].at[part], slot, came.at[at]))
+            leaving.append(pltpu.make_async_copy(slot, targets[n].at[part], left.at[at]))
+    for copy in arriving:
+        copy.start()
+    for copy, onward in zip(arriving, leaving):
+        copy.wait()
+        onward.start()
+    for copy in leaving:
+        copy.wait()
 
 
 def hand_over(arrays):
-    length, parts = arrays[0].shape[0], 4
-    specs = []
-    for a in arrays[:2]:
-        specs.append(pl.BlockSpec((length // parts, a.shape[1]), lambda i: (i, 0)))
-    for a in arrays[2:]:
-        specs.append(pl.BlockSpec(a.shape, lambda i: (0, 0)))
+    anywhere = pl.BlockSpec(memory_space=pl.ANY)
     return pl.pallas_call(
         functools.partial(hand_kernel, len(arrays)),
-        grid=(parts,),
-        in_specs=specs,
-        out_specs=specs,
+        in_specs=[anywhere] * len(arrays),
+        out_specs=[anywhere] * len(arrays),
         out_shape=[jax.ShapeDtypeStruct(a.shape, a.dtype) for a in arrays],
+        scratch_shapes=[pltpu.VMEM(a.shape, a.dtype) for a in arrays]
+        + [pltpu.SemaphoreType.DMA((4 * len(arrays),))] * 2,
         compiler_params=pltpu.CompilerParams(vmem_limit_bytes=56 * 1024 * 1024),
         name="hand_over",
     )(*arrays)

time: 47.1 us -> 39.9 us (0.85)
  Pallas kernels: 45 us -> 37.8 us
    pallas_call x1, Pallas kernels: 41.1 us -> 35.1 us  [run_whole(): pl.pallas_call(functools.partial(whole_kernel, replicas, zeros, scale, sh...]
    pallas_call x1, Pallas kernels: 3.85 us -> 2.7 us  [hand_over(): pl.pallas_call(functools.partial(hand_kernel, len(arrays)), in_specs=[any...]
where the time goes in v5:
time: 39.9 us; the launch traced here: 39.7 us
  Pallas kernels  37.8 us (95%)
  between operations  1.93 us (5%)
    pallas_call x1, Pallas kernels, run_whole(): pl.pallas_call(functools.partial(whole_kernel, replicas, zeros, scale, sh...  35.1 us
    pallas_call x1, Pallas kernels, hand_over(): pl.pallas_call(functools.partial(hand_kernel, len(arrays)), in_specs=[any...  2.7 us

profile of v5, /device:TPU:0, one launch (start us, length us, event | category | flops | bytes accessed | tf_op | source)
XLA Modules:
  0.0 39.7 jit_solution(15529723501697611445)
XLA Ops:
  1.9 35.1 %whole_block.1 = (bf16[128,2048]{1,0:T(8,128)(2,1)}, bf16[128,6144]{1,0:T(8,128)(2,1)}, f32[7,768]{1,0:T(8,128)}, f32[128,128]{1,0:T(8,128)}) custom-call(s32[1]{0:T(128)S(6)} %copy.11.counts, s32[1]{0:T(128)S(6)} %copy.12.plan, s32[1,128]{1,0:T(1,128)} %doc.1, f32[128,128]{1,0:T(8,128)} %taps.1, bf16[7,768]{1,0:T(8,128)(2,1)} %filt.1, ...), custom_call_target="tpu_custom_call" | custom-call | tf_op jit(solution)/shard_map/whole_block/pallas_call | solution.py:470
  37.0 2.7 %hand_over.1 = (bf16[128,2048]{1,0:T(8,128)(2,1)}, bf16[128,6144]{1,0:T(8,128)(2,1)}, f32[7,768]{1,0:T(8,128)}, f32[128,128]{1,0:T(8,128)}) custom-call(bf16[128,2048]{1,0:T(8,128)(2,1)} %get-tuple-element.8.refs_0_, bf16[128,6144]{1,0:T(8,128)(2,1)} %get-tuple-element.9.refs_1_, f32[7,768]{1,0:T(8,128)} %get-tuple-element.10.refs_2_, ...), custom_call_target="tpu_custom_call" | custom-call | tf_op jit(solution)/shard_map/hand_over/pallas_call | solution.py:551

commit v6 on v5

--- a/solution.py
+++ b/solution.py
@@ -257,17 +257,18 @@
         base_back[lines, :] = pltpu.roll(tap_back, a, 1)
         base_rows[lines, :] = pltpu.roll(tap_rows, a, 1)
 
-    def build(block, carry):
-        for i in range(per):
+    def build(pair, carry):
+        for n in range(2 * per):
+            block, i = pair * 2 + n // per, n % per
             at = slice(i * length, (i + 1) * length)
-            tile = pl.ds(pl.multiple_of((block * per + i) * 8, 8), 8)
+            tile = pl.ds(pl.multiple_of((pair * 2 * per + n) * 8, 8), 8)
             one = toeplitz(base_back[tile, :], length)
             forward[block, :, at] = one.astype(BF16) * causal[...]
             two = toeplitz(base_rows[tile, :], length)
             backward[block, :, at] = two.astype(BF16) * causal_t[...]
         return carry
 
-    lax.fori_loop(0, width // LANES, build, 0)
+    lax.fori_loop(0, width // (2 * LANES), build, 0)
     crossing[...] = jnp.zeros_like(crossing)
 
     for copy in gathering:
@@ -288,51 +289,66 @@
     group = lax.broadcasted_iota(jnp.int32, (1, LANES), 1) // gsize
     picks = [(group == i).astype(BF16) for i in range(per)]
 
+    def convolve(n, begin):
+        where = pl.ds(pl.multiple_of(n * width + begin, LANES), WIDE)
+        x = feats[:, where]
+        taps7 = filters[:, where]
+        narrow = taps7.astype(BF16)
+        scaled = jnp.concatenate([x * narrow[j : j + 1] for j in range(1, short)], 0)
+        return taps7[0:1] * x.astype(F32) + dot(down_cat[...], scaled)
+
+    span = crossing.shape[0] * LANES
+
     def blocks(step, carry):
-        def convolve(n):
-            where = pl.ds(pl.multiple_of(n * width + step * WIDE, LANES), WIDE)
-            x = feats[:, where]
-            taps7 = filters[:, where]
-            narrow = taps7.astype(BF16)
-            scaled = jnp.concatenate([x * narrow[j : j + 1] for j in range(1, short)], 0)
-            return taps7[0:1] * x.astype(F32) + dot(down_cat[...], scaled)
-
-        query, key, value = convolve(0), convolve(1), convolve(2)
-        for h in range(WIDE // LANES):
-            cols = slice(h * LANES, (h + 1) * LANES)
-            q, k, v = query[:, cols], key[:, cols], value[:, cols]
-            begin = pl.multiple_of(step * WIDE + h * LANES, LANES)
-            here = pl.ds(begin, LANES)
+        halves = []
+        for sub in range(span // WIDE):
+            begin = step * span + sub * WIDE
+            parts = [convolve(n, begin) for n in range(3)]
+            for h in range(WIDE // LANES):
+                halves.append([p[:, h * LANES : (h + 1) * LANES] for p in parts])
+        products, longs, chosens = [], [], []
+        for h, (q, k, v) in enumerate(halves):
             product = (k * v).astype(BF16)
-            block = step * (WIDE // LANES) + h
-            long_conv = dot(forward[block], jnp.concatenate([product * m for m in picks], 0))
-            alive = living[...]
-            mixed[:, here] = (alive * q * long_conv).astype(BF16)
-            grad_out = cot[:, here].astype(F32) * alive
+            products.append(product)
+            block = step * (span // LANES) + h
+            longs.append(dot(forward[block], jnp.concatenate([product * m for m in picks], 0)))
+        for h, (q, k, v) in enumerate(halves):
+            grad_out = cot[:, here(step, h, 0)].astype(F32) * living[...]
             grad_long = (grad_out * q).astype(BF16)
-            chosen = jnp.concatenate([grad_long * m for m in picks], 0)
-            grad_product = dot(backward[block], chosen)
+            chosens.append(grad_long)
             turned = lax.dot_general(
-                product, flip[...], (((0,), (0,)), ((), ())), preferred_element_type=F32
+                products[h], flip[...], (((0,), (0,)), ((), ())), preferred_element_type=F32
             ).astype(BF16)
             for i in range(per):
                 at = slice(i * gsize, (i + 1) * gsize)
                 crossing[h, at, i * length : (i + 1) * length] = turned[at]
-            crossed = dot(grad_long, crossing[h])
+        for h, (q, k, v) in enumerate(halves):
+            block = step * (span // LANES) + h
+            grad_product = dot(
+                backward[block], jnp.concatenate([chosens[h] * m for m in picks], 0)
+            )
+            grad_short[:, here(step, h, 1)] = (grad_product * v).astype(BF16)
+            grad_short[:, here(step, h, 2)] = (grad_product * k).astype(BF16)
+        for h, (q, k, v) in enumerate(halves):
+            alive = living[...]
+            mixed[:, here(step, h, 0)] = (alive * q * longs[h]).astype(BF16)
+            grad_out = cot[:, here(step, h, 0)].astype(F32) * alive
+            grad_short[:, here(step, h, 0)] = (grad_out * longs[h]).astype(BF16)
+        for h in range(len(halves)):
+            block = step * (span // LANES) + h
+            crossed = dot(chosens[h], crossing[h])
             for i in range(per):
                 part = crossed[:, i * length : (i + 1) * length] * causal_r[...]
                 summed = part[0:8]
                 for at in range(8, length, 8):
                     summed = summed + pltpu.roll(part[at : at + 8], at, 1)
                 med[pl.ds(pl.multiple_of((block * per + i) * 8, 8), 8), :] = summed
-            grad_short[:, here] = (grad_out * long_conv).astype(BF16)
-            there = pl.ds(pl.multiple_of(begin + width, LANES), LANES)
-            grad_short[:, there] = (grad_product * v).astype(BF16)
-            there = pl.ds(pl.multiple_of(begin + 2 * width, LANES), LANES)
-            grad_short[:, there] = (grad_product * k).astype(BF16)
         return carry
 
-    lax.fori_loop(0, width // WIDE, blocks, 0)
+    def here(step, h, n):
+        return pl.ds(pl.multiple_of(n * width + step * span + h * LANES, LANES), LANES)
+
+    lax.fori_loop(0, width // span, blocks, 0)
     save_mixed = pltpu.make_async_copy(mixed, mixed_hbm, loaded.at[2])
     save_mixed.start()
 
@@ -399,18 +415,21 @@
     mparts[place] = total
     medium_two = spread("dp", replicas, lambda peer: mpart, mparts, m2s, m2r)
 
+    bundle = 6
+
     def feats_chunk(index, carry):
-        where = pl.ds(pl.multiple_of(index * WIDE, LANES), WIDE)
-        grad = grad_short[:, where]
-        taps7 = filters[:, where]
-        narrow = taps7.astype(BF16)
-        scaled = jnp.concatenate([grad * narrow[j : j + 1] for j in range(1, short)], 0)
-        total = taps7[0:1] * grad.astype(F32) + dot(up_cat[...], scaled)
-        grads[:, where] = (total * weight).astype(BF16)
+        for sub in range(bundle):
+            where = pl.ds(pl.multiple_of((index * bundle + sub) * WIDE, LANES), WIDE)
+            grad = grad_short[:, where]
+            taps7 = filters[:, where]
+            narrow = taps7.astype(BF16)
+            scaled = jnp.concatenate([grad * narrow[j : j + 1] for j in range(1, short)], 0)
+            total = taps7[0:1] * grad.astype(F32) + dot(up_cat[...], scaled)
+            grads[:, where] = (total * weight).astype(BF16)
         return carry
 
-    pieces = 3 * width // WIDE
-    middle = pieces // 2 * WIDE
+    pieces = 3 * width // WIDE // bundle
+    middle = pieces // 2 * bundle * WIDE
     lax.fori_loop(0, pieces // 2, feats_chunk, 0)
     cols = slice(0, middle)
     save_one = pltpu.make_async_copy(grads.at[:, cols], grads_hbm.at[:, cols], loaded.at[3])
@@ -503,7 +522,7 @@
             pltpu.VMEM(stacked, BF16),
             pltpu.VMEM(stacked, BF16),
             pltpu.VMEM(feats.shape, BF16),
-            pltpu.VMEM((WIDE // LANES, LANES, LANES // gsize * length), BF16),
+            pltpu.VMEM((2 * WIDE // LANES, LANES, LANES // gsize * length), BF16),
             pltpu.VMEM((zeros, depth, groups), BF16),
             pltpu.VMEM((zeros, depth, groups), BF16),
             pltpu.VMEM((depth, groups), F32),

time: 39.9 us -> 35.9 us (0.90)
  Pallas kernels: 37.8 us -> 33.7 us
    pallas_call x1, Pallas kernels: 35.1 us -> 31 us  [run_whole(): pl.pallas_call(functools.partial(whole_kernel, replicas, zeros, scale, sh...]
where the time goes in v6:
time: 35.9 us; the launch traced here: 35.7 us
  Pallas kernels  33.7 us (94%)
  between operations  1.93 us (5%)
    pallas_call x1, Pallas kernels, run_whole(): pl.pallas_call(functools.partial(whole_kernel, replicas, zeros, scale, sh...  31 us
    pallas_call x1, Pallas kernels, hand_over(): pl.pallas_call(functools.partial(hand_kernel, len(arrays)), in_specs=[any...  2.7 us

profile of v6, /device:TPU:0, one launch (start us, length us, event | category | flops | bytes accessed | tf_op | source)
XLA Modules:
  0.0 35.7 jit_solution(2069194925731046092)
XLA Ops:
  1.9 31.0 %whole_block.1 = (bf16[128,2048]{1,0:T(8,128)(2,1)}, bf16[128,6144]{1,0:T(8,128)(2,1)}, f32[7,768]{1,0:T(8,128)}, f32[128,128]{1,0:T(8,128)}) custom-call(s32[1]{0:T(128)S(6)} %copy.11.counts, s32[1]{0:T(128)S(6)} %copy.12.plan, s32[1,128]{1,0:T(1,128)} %doc.1, f32[128,128]{1,0:T(8,128)} %taps.1, bf16[7,768]{1,0:T(8,128)(2,1)} %filt.1, ...), custom_call_target="tpu_custom_call" | custom-call | tf_op jit(solution)/shard_map/whole_block/pallas_call | solution.py:489
  33.0 2.7 %hand_over.1 = (bf16[128,2048]{1,0:T(8,128)(2,1)}, bf16[128,6144]{1,0:T(8,128)(2,1)}, f32[7,768]{1,0:T(8,128)}, f32[128,128]{1,0:T(8,128)}) custom-call(bf16[128,2048]{1,0:T(8,128)(2,1)} %get-tuple-element.8.refs_0_, bf16[128,6144]{1,0:T(8,128)(2,1)} %get-tuple-element.9.refs_1_, f32[7,768]{1,0:T(8,128)} %get-tuple-element.10.refs_2_, ...), custom_call_target="tpu_custom_call" | custom-call | tf_op jit(solution)/shard_map/hand_over/pallas_call | solution.py:570

commit v7 on v6

--- a/solution.py
+++ b/solution.py
@@ -403,9 +403,7 @@
         short_copy(step).start()
         return carry
 
-    lax.fori_loop(1, zeros, send_short, 0)
-    sslots[mine] = short_chunk(mine)
-
+    lax.fori_loop(1, zeros // 2 + 1, send_short, 0)
     for copy in medium_one:
         copy.wait()
     total = mslots[0].astype(F32)
@@ -414,8 +412,18 @@
     mpart[...] = total
     mparts[place] = total
     medium_two = spread("dp", replicas, lambda peer: mpart, mparts, m2s, m2r)
-
-    bundle = 6
+    lax.fori_loop(zeros // 2 + 1, zeros, send_short, 0)
+    sslots[mine] = short_chunk(mine)
+    for copy in medium_two:
+        copy.wait()
+    total = mparts[0]
+    for p in range(1, replicas):
+        total = total + mparts[p]
+    share[...] = total
+    shares[mine] = total
+    medium_three = spread("zero", zeros, lambda peer: share, shares, m3s, m3r)
+
+    bundle = 12
 
     def feats_chunk(index, carry):
         for sub in range(bundle):
@@ -443,14 +451,6 @@
     spart[...] = total
     sparts[place] = total
     short_two = spread("dp", replicas, lambda peer: spart, sparts, s2s, s2r)
-    for copy in medium_two:
-        copy.wait()
-    total = mparts[0]
-    for p in range(1, replicas):
-        total = total + mparts[p]
-    share[...] = total
-    shares[mine] = total
-    medium_three = spread("zero", zeros, lambda peer: share, shares, m3s, m3r)
 
     lax.fori_loop(pieces // 2, pieces, feats_chunk, 0)
     cols = slice(middle, 3 * width)

time: 35.9 us -> 35.9 us (level)
  no operation moved by 1% of the time
where the time goes in v7:
time: 35.9 us; the launch traced here: 35.6 us
  Pallas kernels  33.7 us (94%)
  between operations  1.93 us (5%)
    pallas_call x1, Pallas kernels, run_whole(): pl.pallas_call(functools.partial(whole_kernel, replicas, zeros, scale, sh...  31 us
    pallas_call x1, Pallas kernels, hand_over(): pl.pallas_call(functools.partial(hand_kernel, len(arrays)), in_specs=[any...  2.7 us

profile of v7, /device:TPU:0, one launch (start us, length us, event | category | flops | bytes accessed | tf_op | source)
XLA Modules:
  0.0 35.6 jit_solution(3585271735358565441)
XLA Ops:
  1.9 31.0 %whole_block.1 = (bf16[128,2048]{1,0:T(8,128)(2,1)}, bf16[128,6144]{1,0:T(8,128)(2,1)}, f32[7,768]{1,0:T(8,128)}, f32[128,128]{1,0:T(8,128)}) custom-call(s32[1]{0:T(128)S(6)} %copy.11.counts, s32[1]{0:T(128)S(6)} %copy.12.plan, s32[1,128]{1,0:T(1,128)} %doc.1, f32[128,128]{1,0:T(8,128)} %taps.1, bf16[7,768]{1,0:T(8,128)(2,1)} %filt.1, ...), custom_call_target="tpu_custom_call" | custom-call | tf_op jit(solution)/shard_map/whole_block/pallas_call | solution.py:489
  32.9 2.7 %hand_over.1 = (bf16[128,2048]{1,0:T(8,128)(2,1)}, bf16[128,6144]{1,0:T(8,128)(2,1)}, f32[7,768]{1,0:T(8,128)}, f32[128,128]{1,0:T(8,128)}) custom-call(bf16[128,2048]{1,0:T(8,128)(2,1)} %get-tuple-element.8.refs_0_, bf16[128,6144]{1,0:T(8,128)(2,1)} %get-tuple-element.9.refs_1_, f32[7,768]{1,0:T(8,128)} %get-tuple-element.10.refs_2_, ...), custom_call_target="tpu_custom_call" | custom-call | tf_op jit(solution)/shard_map/hand_over/pallas_call | solution.py:570

commit v8 on v7

--- a/solution.py
+++ b/solution.py
@@ -522,7 +522,7 @@
             pltpu.VMEM(stacked, BF16),
             pltpu.VMEM(stacked, BF16),
             pltpu.VMEM(feats.shape, BF16),
-            pltpu.VMEM((2 * WIDE // LANES, LANES, LANES // gsize * length), BF16),
+            pltpu.VMEM((4 * WIDE // LANES, LANES, LANES // gsize * length), BF16),
             pltpu.VMEM((zeros, depth, groups), BF16),
             pltpu.VMEM((zeros, depth, groups), BF16),
             pltpu.VMEM((depth, groups), F32),

time: 35.9 us -> 35.5 us (0.989)
  Pallas kernels: 33.7 us -> 33.3 us
    pallas_call x1, Pallas kernels: 31 us -> 30.6 us  [run_whole(): pl.pallas_call(functools.partial(whole_kernel, replicas, zeros, scale, sh...]
where the time goes in v8:
time: 35.5 us; the launch traced here: 35.3 us
  Pallas kernels  33.3 us (94%)
  between operations  1.93 us (5%)
    pallas_call x1, Pallas kernels, run_whole(): pl.pallas_call(functools.partial(whole_kernel, replicas, zeros, scale, sh...  30.6 us
    pallas_call x1, Pallas kernels, hand_over(): pl.pallas_call(functools.partial(hand_kernel, len(arrays)), in_specs=[any...  2.7 us

profile of v8, /device:TPU:0, one launch (start us, length us, event | category | flops | bytes accessed | tf_op | source)
XLA Modules:
  0.0 35.3 jit_solution(3080862856821783815)
XLA Ops:
  1.9 30.6 %whole_block.1 = (bf16[128,2048]{1,0:T(8,128)(2,1)}, bf16[128,6144]{1,0:T(8,128)(2,1)}, f32[7,768]{1,0:T(8,128)}, f32[128,128]{1,0:T(8,128)}) custom-call(s32[1]{0:T(128)S(6)} %copy.11.counts, s32[1]{0:T(128)S(6)} %copy.12.plan, s32[1,128]{1,0:T(1,128)} %doc.1, f32[128,128]{1,0:T(8,128)} %taps.1, bf16[7,768]{1,0:T(8,128)(2,1)} %filt.1, ...), custom_call_target="tpu_custom_call" | custom-call | tf_op jit(solution)/shard_map/whole_block/pallas_call | solution.py:489
  32.6 2.7 %hand_over.1 = (bf16[128,2048]{1,0:T(8,128)(2,1)}, bf16[128,6144]{1,0:T(8,128)(2,1)}, f32[7,768]{1,0:T(8,128)}, f32[128,128]{1,0:T(8,128)}) custom-call(bf16[128,2048]{1,0:T(8,128)(2,1)} %get-tuple-element.8.refs_0_, bf16[128,6144]{1,0:T(8,128)(2,1)} %get-tuple-element.9.refs_1_, f32[7,768]{1,0:T(8,128)} %get-tuple-element.10.refs_2_, ...), custom_call_target="tpu_custom_call" | custom-call | tf_op jit(solution)/shard_map/hand_over/pallas_call | solution.py:570
